TPU v7x, 256 devices: a whole 4x4x8 slice. The times are simulated.
256 devices in a mesh: dp: 16 (over y, x), vocab: 16 (over z, core).
Axes of the slice: x: 4, y: 4, z: 8, core: 2. Of those that a mesh axis runs over, the one named last changes fastest.
Arguments:
- hidden: bfloat16 [4096, 3072], P('dp', 'vocab'), may hold values from -64 to 64
- input_grad: bfloat16 [4096, 3072], P('dp', 'vocab'), may hold values from -6 to 6
- embedding: bfloat16 [128256, 3072], P(('dp', 'vocab')), may hold values from -1 to 1
- vocab_proj: bfloat16 [128256, 64], P(('dp', 'vocab')), may hold values from -0.359375 to 0.359375
- feature_proj: bfloat16 [3072, 64], P('vocab'), may hold values from -0.109375 to 0.109375
- token_ids: int32 [4096], P('dp'), may hold values from 0 to 128255
- targets: int32 [4096], P('dp'), may hold values from 0 to 128255
- doc_ids: int32 [4096], P('dp'), may hold values from 0 to 63, as said below
Outputs:
- doc_grads: float32 [64, 4096], P('dp')
Inputs may be any that keep to these rules, and one draw needn't show every extreme that they name: `doc_ids`: never falls; the tokens of group g, positions g * 256 to (g + 1) * 256 - 1, belong to documents g * 4 to (g + 1) * 4 - 1, and each of these documents has one token or more.
All inputs are finite; a program needn't handle non-finite values.
Results may differ from a plain program's by a relative error of at most 0.0003.
Values may be sent and summed in bfloat16 or wider, within the bound.
A program may use at most 128 MiB of HBM per device.

v0:
```python
import jax
import jax.numpy as jnp
from jax import lax
from jax.sharding import PartitionSpec as P

KV = 64
KD = 64
DOC_DP = 4


PRECISE = lax.Precision.HIGHEST


def contract_rows(left_mat, right_mat):
    return lax.dot_general(
        left_mat, right_mat, (((1,), (1,)), ((), ())), preferred_element_type=jnp.float32
    )


def summarize(logits, proj_table):
    local_peak = jnp.max(logits, axis=1)
    scaled = jnp.exp(logits - local_peak[:, None])
    weighted = jnp.dot(scaled, proj_table, precision=PRECISE, preferred_element_type=jnp.float32)
    return (local_peak, jnp.sum(scaled, axis=1), weighted)


def doc_blocks(token_side, feature_side, membership):
    spread = membership[:, :, None] * token_side[:, None, :]
    head_part = jnp.einsum(
        "tdi,tj->dij", spread[:, :, :KV], feature_side[:, :KD], precision=PRECISE
    )
    embed_part = jnp.einsum(
        "tdi,tj->dij", spread[:, :, KV:], feature_side[:, KD:], precision=PRECISE
    )
    return (head_part + embed_part).reshape(membership.shape[1], KV * KD)


def per_device(
    hidden, input_grad, embedding, vocab_proj, feature_proj, token_ids, targets, doc_ids
):
    row_count = embedding.shape[0]
    group_tokens = hidden.shape[0]
    group_count = lax.axis_size("dp")
    shard_count = lax.axis_size("vocab")
    all_tokens = group_tokens * group_count
    group_index = lax.axis_index("dp")
    vocab_index = lax.axis_index("vocab")
    first_row = (group_index * shard_count + vocab_index) * row_count
    proj_table = vocab_proj.astype(jnp.float32)
    full_rows = lax.all_gather(hidden, "vocab", axis=1, tiled=True)
    summary = summarize(
        contract_rows(lax.all_gather(full_rows, "dp", axis=0, tiled=True), embedding), proj_table
    )
    local_peak, local_total, weighted = tuple((fresh for fresh in summary))
    maximum = lax.pmax(local_peak, ("dp", "vocab"))
    rescale = jnp.exp(local_peak - maximum)
    summed_exp = lax.psum(local_total * rescale, ("dp", "vocab"))
    dense_part = weighted * (rescale / summed_exp)[:, None]
    side_terms = jnp.concatenate(
        [
            jnp.dot(hidden, feature_proj, preferred_element_type=jnp.float32),
            jnp.dot(input_grad, feature_proj, preferred_element_type=jnp.float32),
        ],
        axis=1,
    )
    local_docs = doc_ids - group_index * DOC_DP
    doc_numbers = jnp.arange(DOC_DP, dtype=jnp.int32)
    all_ids, all_targets = (
        lax.all_gather(token_ids, "dp", axis=0, tiled=True),
        lax.all_gather(targets, "dp", axis=0, tiled=True),
    )
    columns_here = first_row + jnp.arange(row_count, dtype=jnp.int32)
    one_hot = (jnp.concatenate([all_targets, all_ids])[:, None] == columns_here[None, :]).astype(
        jnp.bfloat16
    )
    looked_up = jnp.dot(one_hot, vocab_proj, preferred_element_type=jnp.float32)
    token_terms = jnp.concatenate(
        [dense_part - looked_up[:all_tokens], looked_up[all_tokens:]], axis=1
    )
    vocab_terms = lax.psum_scatter(token_terms, "dp", scatter_dimension=0, tiled=True)
    token_side, feature_side = lax.psum((vocab_terms, side_terms), "vocab")
    membership = (local_docs[:, None] == doc_numbers[None, :]).astype(jnp.float32)
    return doc_blocks(token_side, feature_side, membership)


def solution(mesh):
    placed = (
        P("dp", "vocab"),
        P("dp", "vocab"),
        P(("dp", "vocab"), None),
        P(("dp", "vocab"), None),
        P("vocab", None),
        P("dp"),
        P("dp"),
        P("dp"),
    )
    return jax.shard_map(
        per_device, mesh=mesh, in_specs=placed, out_specs=P("dp", None), check_vma=False
    )
```

profile of v0, /device:TPU:1, one launch (start us, length us, event | category | flops | bytes accessed | tf_op | source)
XLA Modules:
  0.0 602.3 jit_solution(16098891705814566126)
XLA Ops:
  6.5 0.0 copy-start
  6.5 0.0 all-gather.5.cloned.1.call-start
  6.5 0.7 all-gather.5.cloned.1.call-update
  7.3 0.0 all-gather.7.cloned.1.call-start
  7.3 45.3 %all-gather.5.cloned.1.call-done = bf16[256,3072]{0,1:T(8,128)(2,1)} async-done(((bf16[256,192]{0,1:T(8,128)(2,1)}), bf16[256,3072]{0,1:T(8,128)(2,1)}) %all-gather.5.cloned.1.call-update) | async-done | bytes 1572880 | tf_op jit(solution)/shard_map/all_gather | solution.py:50
  52.6 0.0 all-gather.7.cloned.1.call-update
  52.6 0.0 reduce-scatter.2.cloned.1.call-start
  52.7 17.9 %all-gather = s32[16,1,256]{2,1,0:T(1,128)S(1)} all-gather(s32[1,1,256]{2,1,0:T(1,128)} %bitcast.20), channel_id=1, replica_groups=mesh['dp'=16,'vocab'=16] {'dp'}, dimensions={0}, use_global_device_ids=true | all-gather | bytes 17408 | tf_op jit(solution)/shard_map/all_gather | solution.py:70
  70.5 19.4 %all-gather.1 = s32[16,1,256]{2,1,0:T(1,128)S(1)} all-gather(s32[1,1,256]{2,1,0:T(1,128)} %bitcast.21), channel_id=1, replica_groups=mesh['dp'=16,'vocab'=16] {'dp'}, dimensions={0}, use_global_device_ids=true | all-gather | bytes 17408 | tf_op jit(solution)/shard_map/all_gather | solution.py:69
  90.0 4.2 fusion
  94.2 0.0 copy-start.1
  94.2 1.3 copy-done.1
  95.5 125.7 %all-gather.7.cloned.1.call-done = bf16[4096,3072]{0,1:T(8,128)(2,1)} async-done(((bf16[256,3072]{0,1:T(8,128)(2,1)}), bf16[4096,3072]{0,1:T(8,128)(2,1)}) %all-gather.7.cloned.1.call-update) | async-done | bytes 25165840 | tf_op jit(solution)/shard_map/all_gather | solution.py:52
  221.2 0.0 copy-done
  221.2 19.8 %fusion.15 = (f32[4096]{0:T(1024)S(1)}, f32[4096,501]{0,1:T(8,128)}) fusion(bf16[4096,3072]{0,1:T(8,128)(2,1)} %all-gather.7.cloned.1.call-done, bf16[501,3072]{1,0:T(8,128)(2,1)S(1)} %copy-done), kind=kOutput, calls=%fused_computation.27 | convolution fusion | flops 12610125824 | bytes 36468736 | tf_op jit(solution)/shard_map/dot_general | solution.py:15
  241.0 0.0 copy-start.5
  241.0 76.4 %pmax.7 = f32[4096]{0:T(1024)S(1)} all-reduce(f32[4096]{0:T(1024)S(1)} %get-tuple-element.7), channel_id=1, replica_groups=mesh['dp'=16,'vocab'=16] {'dp','vocab'}, use_global_device_ids=true, to_apply=%region_1.0 | all-reduce | flops 4096 | bytes 32768 | tf_op jit(solution)/shard_map/pmax | solution.py:55
  317.4 4.5 fusion.4
  321.9 74.0 %psum.21 = f32[4096]{0:T(1024)S(1)} all-reduce(f32[4096]{0:T(1024)S(1)} %fusion.13), channel_id=1, replica_groups=mesh['dp'=16,'vocab'=16] {'dp','vocab'}, use_global_device_ids=true, to_apply=%region_3.0 | all-reduce | flops 4096 | bytes 32768 | tf_op jit(solution)/shard_map/psum | solution.py:57
  395.9 0.0 slice-start
  395.9 0.0 copy-done.5
  395.9 0.0 copy-start.2
  395.9 0.0 copy-start.3
  396.0 0.0 copy-start.4
  396.0 0.0 copy-start.6
  396.0 8.2 %fusion.7 = f32[4096,64]{0,1:T(8,128)S(1)} fusion(bf16[501,64]{0,1:T(8,128)(2,1)S(1)} %copy-done.5, f32[4096,501]{0,1:T(8,128)} %get-tuple-element.8, f32[4096]{0:T(1024)S(1)} %get-tuple-element.7, f32[8192,64]{0,1:T(8,128)} %copy-done.1, f32[4096]{0:T(1024)S(1)} %fusion.12), kind=kOutput, calls=%fused_computation.8 | convolution fusion | flops 1578586112 | bytes 10402432 | tf_op jit(solution)/shard_map/dot_general | solution.py:23
  404.2 0.0 slice-done
  404.2 1.5 pad_maximum_fusion
  405.7 0.0 reduce-scatter.2.cloned.1.call-update
  405.7 0.0 all-reduce.3.cloned.1.call-start
  405.8 0.0 copy-done.2
  405.8 0.0 copy-done.3
  405.8 0.1 fusion.16
  405.9 0.0 copy-done.4
  405.9 0.1 fusion.17
  406.1 0.7 pad_maximum_fusion.1
  406.7 0.0 copy-done.6
  406.7 72.8 %reduce-scatter.2.cloned.1.call-done = f32[256,128]{0,1:T(8,128)} async-done(((f32[4096,128]{0,1:T(8,128)}), f32[256,128]{0,1:T(8,128)}) %reduce-scatter.2.cloned.1.call-update) | async-done | bytes 131088 | tf_op jit(solution)/shard_map/reduce_scatter | solution.py:80
  479.6 0.0 all-reduce.3.cloned.1.call-update
  479.6 112.0 %all-reduce.3.cloned.1.call-done = (f32[256,128]{0,1:T(8,128)}, f32[256,128]{0,1:T(8,128)}) async-done(((f32[256,128]{0,1:T(8,128)}, f32[256,128]{0,1:T(8,128)}), (f32[256,128]{0,1:T(8,128)}, f32[256,128]{0,1:T(8,128)})) %all-reduce.3.cloned.1.call-update) | async-done | bytes 262160 | tf_op jit(solution)/shard_map/psum | solution.py:81
  591.6 0.9 broadcast_multiply_fusion
  592.6 1.2 fusion.10
  593.8 1.2 convolution_add_fusion
  595.0 0.7 reshape.33
  (6 shorter events, 0.0 us)
Async XLA Ops:
  6.5 214.7 %copy-start = (bf16[501,3072]{1,0:T(8,128)(2,1)S(1)}, bf16[501,3072]{1,0:T(8,128)(2,1)}, u32[]{:S(2)}) copy-start(bf16[501,3072]{1,0:T(8,128)(2,1)} %param.10) | copy-start | bytes 9234436
  6.5 46.0 %all-gather.5.cloned.1.call-start = ((), (), s32[]{:S(2)}) async-start(), calls=%async_computation.1 | async-start | bytes 1671168 | tf_op jit(solution)/shard_map/all_gather | solution.py:50
  7.3 213.9 %all-gather.7.cloned.1.call-start = ((), (), s32[]{:S(2)}) async-start(), calls=%async_computation.2 | async-start | bytes 26738688 | tf_op jit(solution)/shard_map/all_gather | solution.py:52
  52.6 427.0 %reduce-scatter.2.cloned.1.call-start = ((), (), s32[]{:S(2)}) async-start(), calls=%async_computation.3 | async-start | bytes 2228224 | tf_op jit(solution)/shard_map/reduce_scatter | solution.py:80
  94.2 1.3 copy-start.1
  241.0 154.9 %copy-start.5 = (bf16[501,64]{0,1:T(8,128)(2,1)S(1)}, bf16[501,64]{0,1:T(8,128)(2,1)}, u32[]{:S(2)}) copy-start(bf16[501,64]{0,1:T(8,128)(2,1)} %param.11) | copy-start | bytes 192388
  395.9 8.3 %slice-start = ((f32[8192,64]{0,1:T(8,128)}), f32[4096,64]{0,1:T(8,128)S(1)}, s32[]{:S(2)}) async-start(f32[8192,64]{0,1:T(8,128)} %copy-done.1), calls=%async_computation.5 | async-start | bytes 2097152 | tf_op jit(solution)/shard_map/slice | solution.py:78
  395.9 9.8 %copy-start.2 = (bf16[256,192]{0,1:T(8,128)(2,1)S(1)}, bf16[256,192]{0,1:T(8,128)(2,1)}, u32[]{:S(2)}) copy-start(bf16[256,192]{0,1:T(8,128)(2,1)} %param.8) | copy-start | bytes 294916
  395.9 9.8 %copy-start.3 = (bf16[192,64]{0,1:T(8,128)(2,1)S(1)}, bf16[192,64]{0,1:T(8,128)(2,1)}, u32[]{:S(2)}) copy-start(bf16[192,64]{0,1:T(8,128)(2,1)} %param.12) | copy-start | bytes 73732
  396.0 9.9 %copy-start.4 = (bf16[256,192]{0,1:T(8,128)(2,1)S(1)}, bf16[256,192]{0,1:T(8,128)(2,1)}, u32[]{:S(2)}) copy-start(bf16[256,192]{0,1:T(8,128)(2,1)} %param.9) | copy-start | bytes 294916
  396.0 10.8 %copy-start.6 = (s32[256]{0:T(256)S(1)}, s32[256]{0:T(256)}, u32[]{:S(2)}) copy-start(s32[256]{0:T(256)} %param.15) | copy-start | bytes 3076
  405.7 185.9 %all-reduce.3.cloned.1.call-start = ((), (), s32[]{:S(2)}) async-start(), calls=%async_computation.4 | async-start | bytes 524288 | tf_op jit(solution)/shard_map/psum | solution.py:81
Sparse Core Ops, SparseCore 0:
  9.2 43.3 all-gather.4
  55.0 166.1 all-gather.6
  405.8 73.6 reduce-scatter.1
  481.9 109.7 all-reduce.2
where the time goes:
time: 603 us; the launch traced here: 602 us
  waiting for transfers between devices  357 us (59%)
  blocking collectives  188 us (31%)
  matrix products  34.9 us (6%)
  between operations  13.3 us (2%)
  other arithmetic  7.6 us (1%)
    all_gather x1, waiting for transfers between devices, per_device(): lax.all_gather(full_rows, 'dp', axis=0, tiled=True)  126 us
    psum x1, waiting for transfers between devices, per_device(): token_side, feature_side = lax.psum((vocab_terms, side_terms), 'vocab')  112 us
    pmax x1, blocking collectives, per_device(): maximum = lax.pmax(local_peak, ('dp', 'vocab'))  76.4 us
    psum x1, blocking collectives, per_device(): summed_exp = lax.psum(local_total * rescale, ('dp', 'vocab'))  74 us
    reduce_scatter x1, waiting for transfers between devices, per_device(): lax.psum_scatter(token_terms, 'dp', scatter_dimension=0, tiled=True)  72.8 us
    all_gather x1, waiting for transfers between devices, per_device(): full_rows = lax.all_gather(hidden, 'vocab', axis=1, tiled=True)  45.3 us
    dot_general x1, matrix products, contract_rows(): lax.dot_general(left_mat, right_mat, (((1,), (1,)), ((), ())), preferred_...  19.8 us
    all_gather x1, blocking collectives, per_device(): lax.all_gather(token_ids, 'dp', axis=0, tiled=True)  19.4 us
  transfers between devices with their start and end apart: 4, of which 4 were waited for; matrix products, arithmetic and copies ran while one was open for 1% of the time, Pallas kernels for 0%

commit v1 on v0

v1 whole, which is shorter than its diff:
```python
import jax
import jax.numpy as jnp
from jax import lax
from jax.experimental import pallas as pl
from jax.experimental.pallas import tpu as pltpu
from jax.sharding import PartitionSpec as P

MESH = pl.DeviceIdType.MESH
PRECISE = lax.Precision.HIGHEST
V_ROWS = 501
PAD_ROWS = 512
D = 3072
SLICE = 384
NEAR = ((1, 1), (2, 2), (3, 3))


def logits_of(tokens, rows):
    return lax.dot_general(
        tokens, rows, (((1,), (1,)), ((), ())), preferred_element_type=jnp.float32
    )


def mix(parts):
    peaks = [part[:, 65:66] for part in parts]
    top = peaks[0]
    for peak in peaks[1:]:
        top = jnp.maximum(top, peak)
    total = parts[0] * jnp.exp(peaks[0] - top)
    for part, peak in zip(parts[1:], peaks[1:]):
        total = total + part * jnp.exp(peak - top)
    lane = lax.broadcasted_iota(jnp.int32, total.shape, 1)
    return jnp.where(lane == 65, top, total)


def kernel(
    hid_ref, grad_ref, fp_ref, pe_ref, tgt_ref, ids_ref, docs_ref, emb_ref, out_ref,
    rx, gath, hall, emb, pe, pet, idb, part, look, look_in, part_in, q1, q1_in, q2, q2_in, tok, feat, side, side_in, sd_in, sz, sz_in,
    sem_l, sem_c, sem_z, sem_1, sem_2, sem_i, sem_s, sem_r, sem_q, sem_t,
):
    g, v = lax.axis_index("dp"), lax.axis_index("vocab")
    x, y = lax.rem(g, 4), lax.div(g, 4)
    z, c = lax.div(v, 2), lax.rem(v, 2)

    def dev(dx=0, dy=0, dz=0, dc=0):
        return (
            lax.rem(y + dy, 4) * 4 + lax.rem(x + dx, 4),
            lax.rem(z + dz, 8) * 2 + lax.rem(c + dc, 2),
        )

    def remote(src, dst, send, recv, to):
        return pltpu.make_async_remote_copy(
            src_ref=src, dst_ref=dst, send_sem=send, recv_sem=recv, device_id=to, device_id_type=MESH
        )

    started = []

    def go(copy):
        copy.start()
        started.append(copy)
        return copy

    emb_local = pltpu.make_async_copy(emb_ref, emb.at[c], sem_l.at[0])
    emb_local.start()
    pe[c] = pe_ref[...]
    first = c == 0
    row_id = lax.broadcasted_iota(jnp.int32, (8, 128), 0)
    own_tgt = jnp.where(first, tgt_ref[0:1], tgt_ref[1:2])
    own_ids = jnp.where(first, ids_ref[0:1], ids_ref[1:2])
    idb[y, x] = jnp.where(row_id == 0, own_tgt, own_ids)

    barrier = pltpu.get_barrier_semaphore()
    peers = [dev(dc=1)] + [dev(dz=k) for k in range(1, 8)]
    peers += [dev(dx=k) for k in range(1, 4)] + [dev(dy=k) for k in range(1, 4)]
    for peer in peers:
        pl.semaphore_signal(barrier, inc=1, device_id=peer, device_id_type=MESH)
    pl.semaphore_wait(barrier, len(peers))

    other = pl.multiple_of((1 - c) * 128, 128)
    mine = pl.multiple_of(c * 128, 128)
    swap = go(remote(hid_ref.at[pl.ds(other, 128)], rx, sem_c.at[0], sem_c.at[1], dev(dc=1)))
    ids_1 = [
        go(remote(idb.at[y, x], idb.at[y, x], sem_i.at[0, 0, k - 1], sem_i.at[0, 1, k - 1], dev(dx=k)))
        for k in range(1, 4)
    ]
    pe_swap = go(remote(pe.at[c], pe.at[c], sem_c.at[2], sem_c.at[3], dev(dc=1)))
    swap.wait_recv()
    own_half, got_half = hid_ref[pl.ds(mine, 128), :], rx[...]
    left = jnp.where(first, own_half, got_half)
    right = jnp.where(first, got_half, own_half)

    def columns(zz):
        return pl.ds(pl.multiple_of(lax.rem(zz, 8) * SLICE, 128), SLICE)

    gath[:, columns(z)] = jnp.concatenate([left, right], axis=1)

    def ring(direction, step):
        if direction == 0:
            where, to = columns(z + 8 - (step - 1)), dev(dz=1)
        else:
            where, to = columns(z + step - 1), dev(dz=7)
        block = gath.at[:, where]
        return remote(block, block, sem_z.at[direction, 0, step - 1], sem_z.at[direction, 1, step - 1], to)

    rings = {}
    for direction in (0, 1):
        rings[direction, 1] = go(ring(direction, 1))
    emb_swap = go(remote(emb_ref, emb.at[c], sem_c.at[4], sem_c.at[5], dev(dc=1)))

    side[:, :64] = jnp.dot(hid_ref[...], fp_ref[...], preferred_element_type=jnp.float32)
    side[:, 64:] = jnp.dot(grad_ref[...], fp_ref[...], preferred_element_type=jnp.float32)
    side_swap = go(remote(side.at[pl.ds(other, 128)], sd_in, sem_c.at[6], sem_c.at[7], dev(dc=1)))

    for step in range(1, 4):
        for direction in (0, 1):
            rings[direction, step].wait_recv()
            if step < 3 or direction == 0:
                rings[direction, step + 1] = go(ring(direction, step + 1))
        if step == 1:
            for copy in ids_1:
                copy.wait_recv()
            ids_2 = [
                go(remote(idb.at[y], idb.at[y], sem_i.at[1, 0, k - 1], sem_i.at[1, 1, k - 1], dev(dy=k)))
                for k in range(1, 4)
            ]
        if step == 2:
            side_swap.wait_recv()
            both = side[pl.ds(mine, 128), :] + sd_in[...]
            for zz in range(8):
                for half in range(2):
                    sz[zz, half] = both[half * 64 + zz * 8 : half * 64 + zz * 8 + 8]
            side_z = [
                go(remote(sz.at[lax.rem(z + k, 8)], sz_in.at[k], sem_s.at[0, 0, k - 1], sem_s.at[0, 1, k - 1], dev(dz=k)))
                for k in range(1, 8)
            ]
    rings[0, 4].wait_recv()

    out_at, in_at = (y, x), (x, y)

    def inner(half, k):
        return dev(dx=k) if half == 0 else dev(dy=k)

    def outer(half, k):
        return dev(dy=k) if half == 0 else dev(dx=k)

    STEP = (1, 3)

    def first_own(half, way):
        return remote(
            gath.at[pl.ds(half * 64, 64)], hall.at[half, out_at[half], in_at[half]],
            sem_1.at[half, way, 0, 0], sem_1.at[half, way, 1, 0], inner(half, STEP[way]),
        )

    def first_on(half, way):
        from_pos = lax.rem(in_at[half] + 4 - STEP[way], 4)
        block = hall.at[half, out_at[half], from_pos, pl.ds(way * 32, 32)]
        return remote(block, block, sem_1.at[half, way, 0, 1], sem_1.at[half, way, 1, 1], inner(half, STEP[way]))

    def second_own(half, way, k):
        pos = lax.rem(in_at[half] + k, 4)
        dst = hall.at[half, out_at[half], pos]
        src = gath.at[pl.ds(half * 64, 64)] if k == 0 else dst
        return remote(src, dst, sem_2.at[half, way, 0, 0, k], sem_2.at[half, way, 1, 0, k], outer(half, STEP[way]))

    def second_on(half, way, k):
        pos = lax.rem(in_at[half] + k, 4)
        from_row = lax.rem(out_at[half] + 4 - STEP[way], 4)
        block = hall.at[half, from_row, pos, pl.ds(way * 32, 32)]
        return remote(
            block, block, sem_2.at[half, way, 0, 1, k], sem_2.at[half, way, 1, 1, k], outer(half, STEP[way])
        )

    HALVES, WAYS = (0, 1), (0, 1)
    near = {(h, w): go(first_own(h, w)) for h in HALVES for w in WAYS}
    for h in HALVES:
        for w in WAYS:
            go(second_own(h, w, 0))
    keep = [
        pltpu.make_async_copy(gath.at[pl.ds(h * 64, 64)], hall.at[h, out_at[h], in_at[h]], sem_l.at[1 + h])
        for h in HALVES
    ]
    for copy in keep:
        copy.start()

    pe_swap.wait_recv()
    for b in range(2):
        pet[b] = jnp.transpose(pe[b].astype(jnp.float32)).astype(jnp.bfloat16)

    far = {}
    for h in HALVES:
        for w in WAYS:
            near[h, w].wait_recv()
            far[h, w] = go(first_on(h, w))
    for k in (1, 3):
        for h in HALVES:
            for w in WAYS:
                go(second_own(h, w, k))

    sz_in[0] = sz[z]
    for copy in side_z:
        copy.wait_recv()
    total = sz_in[0]
    for k in range(1, 8):
        total = total + sz_in[k]
    feat[c, :, z] = total
    feat_z = [
        go(remote(feat.at[c, :, z], feat.at[c, :, z], sem_s.at[1, 0, k - 1], sem_s.at[1, 1, k - 1], dev(dz=k)))
        for k in range(1, 8)
    ]

    for h in HALVES:
        for w in WAYS:
            far[h, w].wait_recv()
    for h in HALVES:
        for w in WAYS:
            go(second_own(h, w, 2))
    for copy in feat_z:
        copy.wait_recv()
    feat_swap = go(remote(feat.at[c], feat.at[c], sem_c.at[8], sem_c.at[9], dev(dc=1)))

    for copy in ids_2:
        copy.wait_recv()
    row_base = (g * 16 + z * 2) * V_ROWS

    def look_up(group, carry):
        gy, gx = lax.div(group, 4), lax.rem(group, 4)
        ids = idb[gy, gx]
        wanted = jnp.concatenate([ids[0:1], ids[1:2]], axis=1) - row_base
        found = None
        for b in range(2):
            numbers = lax.broadcasted_iota(jnp.int32, (PAD_ROWS, 256), 0) + b * V_ROWS
            hit = jnp.where(numbers == wanted, 1.0, 0.0).astype(jnp.bfloat16)
            term = jnp.dot(pet[b, :64], hit, preferred_element_type=jnp.float32)
            found = term if found is None else found + term
        stacked = jnp.concatenate([found[:, :128], found[:, 128:]], axis=0)
        rows = jnp.transpose(stacked).astype(jnp.bfloat16)
        look[0, gy, gx] = rows[:64]
        look[1, gx, gy] = rows[64:]
        return carry

    lax.fori_loop(0, 16, look_up, 0)

    def look_send(half, k):
        return remote(
            look.at[half, lax.rem(out_at[half] + k, 4)], look_in.at[half, k - 1],
            sem_r.at[0, half, 0, k - 1], sem_r.at[0, half, 1, k - 1], outer(half, k),
        )

    look_sends = [go(look_send(h, k)) for h in HALVES for k in (1, 2, 3)]

    for copy in keep:
        copy.wait()
    emb_local.wait()
    emb_swap.wait_recv()

    def part_send(t, half, k, to):
        return remote(
            part.at[t], part_in.at[half, k - 1], sem_r.at[1, half, 0, k - 1], sem_r.at[1, half, 1, k - 1], to
        )

    def tile(t, carry):
        half, turn = lax.rem(t, 2), lax.div(t, 2)
        k = turn + lax.div(turn, 2) - 2 * lax.div(turn, 3)

        @pl.when(t == 2)
        def _():
            for kk in (0, 1, 3, 2):
                for h in HALVES:
                    for w in WAYS:
                        second_own(h, w, kk).wait_recv()
                        second_on(h, w, kk).start()

        @pl.when(t == 6)
        def _():
            for kk in (0, 1, 3, 2):
                for w in WAYS:
                    second_on(0, w, kk).wait_recv()

        @pl.when(t == 7)
        def _():
            for kk in (0, 1, 3, 2):
                for w in WAYS:
                    second_on(1, w, kk).wait_recv()

        row = lax.rem(y * (1 - half) + x * half + k, 4)
        tokens = hall[half, row].reshape(256, D)
        l0 = logits_of(tokens, emb[0])
        l1 = logits_of(tokens, emb[1])
        top = jnp.maximum(jnp.max(l0, axis=1, keepdims=True), jnp.max(l1, axis=1, keepdims=True))
        acc = None
        for b, logits in enumerate((l0, l1)):
            scaled = jnp.exp(logits - top)
            coarse = scaled.astype(jnp.bfloat16)
            fine = (scaled - coarse.astype(jnp.float32)).astype(jnp.bfloat16)
            table = pe[b, :V_ROWS]
            for piece in (coarse, fine):
                term = jnp.dot(piece, table, preferred_element_type=jnp.float32)
                acc = term if acc is None else acc + term
        lane = lax.broadcasted_iota(jnp.int32, acc.shape, 1)
        part[t] = jnp.where(lane == 65, top, acc)

        @pl.when(turn > 0)
        def _():
            part_send(t, half, k, dev(dx=half * k, dy=(1 - half) * k)).start()

        return carry

    lax.fori_loop(0, 8, tile, 0)

    for copy in look_sends:
        copy.wait_recv()
    for h in HALVES:
        for k in (1, 2, 3):
            part_send(0, h, k, outer(h, k)).wait_recv()
        mixed = mix([part[h]] + [part_in[h, k] for k in range(3)])
        looked = look[h, out_at[h]].astype(jnp.float32)
        for k in range(3):
            looked = looked + look_in[h, k].astype(jnp.float32)
        q1[h, :, :, :128] = mixed.reshape(4, 64, 128)
        q1[h, :, :, 128:] = looked
        for k in (1, 2, 3):
            go(
                remote(
                    q1.at[h, lax.rem(in_at[h] + k, 4)], q1_in.at[h, k - 1],
                    sem_q.at[h, 0, k - 1], sem_q.at[h, 1, k - 1], inner(h, k),
                )
            )
    for h in HALVES:
        for k in (1, 2, 3):
            remote(q1.at[h, 0], q1_in.at[h, k - 1], sem_q.at[h, 0, k - 1], sem_q.at[h, 1, k - 1], inner(h, k)).wait_recv()
        own = q1[h, in_at[h]]
        mixed = mix([own[:, :128]] + [q1_in[h, k, :, :128] for k in range(3)])
        looked = own[:, 128:]
        for k in range(3):
            looked = looked + q1_in[h, k, :, 128:]
        q2[:, h, :, :128] = mixed.reshape(8, 8, 128)
        q2[:, h, :, 128:] = looked.reshape(8, 8, 128)
    q2_z = [
        go(remote(q2.at[lax.rem(z + k, 8)], q2_in.at[k - 1], sem_t.at[0, 0, k - 1], sem_t.at[0, 1, k - 1], dev(dz=k)))
        for k in range(1, 8)
    ]
    for copy in q2_z:
        copy.wait_recv()
    sums = [q2[z].reshape(16, 256)] + [q2_in[k].reshape(16, 256) for k in range(7)]
    mixed = mix([one[:, :128] for one in sums])
    looked = sums[0][:, 128:]
    for one in sums[1:]:
        looked = looked + one[:, 128:]
    head = mixed[:, :64] / mixed[:, 64:65] - looked[:, :64]
    tok[c, :, z] = jnp.concatenate([head, looked[:, 64:]], axis=1).reshape(2, 8, 128)
    tok_z = [
        go(remote(tok.at[c, :, z], tok.at[c, :, z], sem_t.at[1, 0, k - 1], sem_t.at[1, 1, k - 1], dev(dz=k)))
        for k in range(1, 8)
    ]
    for copy in tok_z:
        copy.wait_recv()
    tok_swap = go(remote(tok.at[c], tok.at[c], sem_c.at[10], sem_c.at[11], dev(dc=1)))
    feat_swap.wait_recv()
    tok_swap.wait_recv()

    turned = jnp.transpose(tok[...].reshape(256, 128))
    local = jnp.concatenate([docs_ref[0:1], docs_ref[1:2]], axis=1) - g * 4
    feats = feat[...].reshape(256, 128)
    member = [jnp.where(local == d, 1.0, 0.0) for d in range(4)]
    head_lhs = jnp.concatenate([turned[:64] * m for m in member], axis=0)
    embed_lhs = jnp.concatenate([turned[64:] * m for m in member], axis=0)
    out_ref[...] = jnp.dot(
        head_lhs, feats[:, :64], precision=PRECISE, preferred_element_type=jnp.float32
    ) + jnp.dot(embed_lhs, feats[:, 64:], precision=PRECISE, preferred_element_type=jnp.float32)

    for copy in started:
        copy.wait_send()
    for h in HALVES:
        for w in WAYS:
            for k in range(4):
                second_on(h, w, k).wait_send()
        for k in (1, 2, 3):
            part_send(0, h, k, outer(h, k)).wait_send()


def per_device(hidden, input_grad, embedding, vocab_proj, feature_proj, token_ids, targets, doc_ids):
    table = jnp.concatenate(
        [vocab_proj, jnp.ones((V_ROWS, 1), jnp.bfloat16), jnp.zeros((V_ROWS, 63), jnp.bfloat16)], axis=1
    )
    table = jnp.pad(table, ((0, PAD_ROWS - V_ROWS), (0, 0)))
    vmem = pl.BlockSpec(memory_space=pltpu.VMEM)
    bf16, f32, i32 = jnp.bfloat16, jnp.float32, jnp.int32
    dma = pltpu.SemaphoreType.DMA
    out = pl.pallas_call(
        kernel,
        out_shape=jax.ShapeDtypeStruct((256, 64), f32),
        in_specs=[vmem] * 7 + [pl.BlockSpec(memory_space=pl.ANY)],
        out_specs=vmem,
        scratch_shapes=[
            pltpu.VMEM((128, 192), bf16),
            pltpu.VMEM((128, D), bf16),
            pltpu.VMEM((2, 4, 4, 64, D), bf16),
            pltpu.VMEM((2, V_ROWS, D), bf16),
            pltpu.VMEM((2, PAD_ROWS, 128), bf16),
            pltpu.VMEM((2, 128, PAD_ROWS), bf16),
            pltpu.VMEM((4, 4, 8, 128), i32),
            pltpu.VMEM((8, 256, 128), f32),
            pltpu.VMEM((2, 4, 4, 64, 128), bf16),
            pltpu.VMEM((2, 3, 4, 64, 128), bf16),
            pltpu.VMEM((2, 3, 256, 128), f32),
            pltpu.VMEM((2, 4, 64, 256), f32),
            pltpu.VMEM((2, 3, 64, 256), f32),
            pltpu.VMEM((8, 2, 8, 256), f32),
            pltpu.VMEM((7, 2, 8, 256), f32),
            pltpu.VMEM((2, 2, 8, 8, 128), f32),
            pltpu.VMEM((2, 2, 8, 8, 128), f32),
            pltpu.VMEM((256, 128), f32),
            pltpu.VMEM((8, 2, 8, 128), f32),
            pltpu.VMEM((128, 128), f32),
            pltpu.VMEM((8, 2, 8, 128), f32),
            pltpu.VMEM((8, 2, 8, 128), f32),
            dma((3,)),
            dma((12,)),
            dma((2, 2, 4)),
            dma((2, 2, 2, 2)),
            dma((2, 2, 2, 2, 4)),
            dma((2, 2, 3)),
            dma((2, 2, 7)),
            dma((2, 2, 2, 3)),
            dma((2, 2, 3)),
            dma((2, 2, 7)),
        ],
        compiler_params=pltpu.CompilerParams(
            collective_id=0, has_side_effects=True, vmem_limit_bytes=60 * 2**20
        ),
        name="doc_grads",
    )(
        hidden, input_grad, feature_proj, table,
        targets.reshape(2, 128), token_ids.reshape(2, 128), doc_ids.reshape(2, 128), embedding,
    )
    return out.reshape(4, 4096)


def solution(mesh):
    placed = (
        P("dp", "vocab"),
        P("dp", "vocab"),
        P(("dp", "vocab"), None),
        P(("dp", "vocab"), None),
        P("vocab", None),
        P("dp"),
        P("dp"),
        P("dp"),
    )
    return jax.shard_map(
        per_device, mesh=mesh, in_specs=placed, out_specs=P("dp", None), check_vma=False
    )
```

time: 603 us -> 134 us (0.22)
  waiting for transfers between devices: 357 us -> 0 us
  blocking collectives: 188 us -> 0 us
  Pallas kernels: 0 us -> 126 us
  matrix products: 34.9 us -> 0 us
  between operations: 13.3 us -> 0.02 us
  other arithmetic: 7.6 us -> 0.05 us
  local copies, waits for them, and re-layouts: 2.07 us -> 8.22 us
    all_gather x2 -> x0, waiting for transfers between devices: 171 us -> none  [the longest x1 126 us: per_device(): lax.all_gather(full_rows, 'dp', axis=0, tiled=True)]
    pallas_call x0 -> x1, Pallas kernels: none -> 126 us  [per_device(): pl.pallas_call(kernel, out_shape=jax.ShapeDtypeStruct((256, 64), f32), in...]
    psum x1 -> x0, waiting for transfers between devices: 112 us -> none  [per_device(): token_side, feature_side = lax.psum((vocab_terms, side_terms), 'vocab')]
    pmax x1 -> x0, blocking collectives: 76.4 us -> none  [per_device(): maximum = lax.pmax(local_peak, ('dp', 'vocab'))]
    psum x1 -> x0, blocking collectives: 74 us -> none  [per_device(): summed_exp = lax.psum(local_total * rescale, ('dp', 'vocab'))]
    reduce_scatter x1 -> x0, waiting for transfers between devices: 72.8 us -> none  [per_device(): lax.psum_scatter(token_terms, 'dp', scatter_dimension=0, tiled=True)]
    all_gather x2 -> x0, blocking collectives: 37.3 us -> none  [the longest x1 19.4 us: per_device(): lax.all_gather(token_ids, 'dp', axis=0, tiled=True)]
    dot_general x7 -> x0, matrix products: 34.9 us -> none  [the longest x1 19.8 us: contract_rows(): lax.dot_general(left_mat, right_mat, (((1,), (1,)), ((), ())), preferred_...]
  transfers between devices with their start and end apart: 4 -> 0, of which waited for: 4 -> 0; matrix products, arithmetic and copies ran while one was open for 1% -> 0% of each run, Pallas kernels for 0% -> 0%
where the time goes in v1:
time: 134 us
  Pallas kernels  126 us (94%)
  local copies, waits for them, and re-layouts  8.22 us (6%)
    pallas_call x1, Pallas kernels, per_device(): pl.pallas_call(kernel, out_shape=jax.ShapeDtypeStruct((256, 64), f32), in...  126 us
    unnamed x4, local copies, waits for them, and re-layouts  5.75 us

profile of v1, /device:TPU:1, one launch (start us, length us, event | category | flops | bytes accessed | tf_op | source)
XLA Modules:
  0.0 134.2 jit_solution(4566949144778613498)
XLA Ops:
  0.0 0.1 pad.6.clone
  0.1 0.1 pad.7.clone
  0.2 1.5 %copy.16.fp_ref = bf16[192,64]{1,0:T(8,128)(2,1)} copy(bf16[192,64]{0,1:T(8,128)(2,1)} %param.12) | data formatting | bytes 49152 | tf_op args[4]
  1.6 1.0 copy.13
  2.6 0.1 maximum_maximum_fusion
  2.7 0.7 pad.4.pe_ref
  3.4 1.6 %copy.14.hid_ref = bf16[256,192]{1,0:T(8,128)(2,1)} copy(bf16[256,192]{0,1:T(8,128)(2,1)} %param.8) | data formatting | bytes 196608 | tf_op args[0]
  5.0 1.6 %copy.15.grad_ref = bf16[256,192]{1,0:T(8,128)(2,1)} copy(bf16[256,192]{0,1:T(8,128)(2,1)} %param.9) | data formatting | bytes 196608 | tf_op args[1]
  6.6 125.9 %doc_grads.1 = f32[256,64]{1,0:T(8,128)} custom-call(bf16[256,192]{1,0:T(8,128)(2,1)} %copy.14.hid_ref, bf16[256,192]{1,0:T(8,128)(2,1)} %copy.15.grad_ref, bf16[192,64]{1,0:T(8,128)(2,1)} %copy.16.fp_ref, bf16[512,128]{1,0:T(8,128)(2,1)} %pad.4.pe_ref, s32[2,128]{1,0:T(2,128)} %bitcast.4, s32[2,128]{1,0:T(2,128)} %bitcast.5, s32[2,128]{1,0:T(2,128)} %bitcast.6, ...), custom_call_target="tpu_custom_call" | custom-call | tf_op jit(solution)/shard_map/doc_grads/pallas_call | solution.py:388
  132.5 1.6 %reshape.15 = f32[4,4096]{1,0:T(4,128)} reshape(f32[256,64]{1,0:T(8,128)} %doc_grads.1) | data formatting | bytes 131072 | tf_op jit(solution)/shard_map/reshape | solution.py:435
  (1 shorter events, 0.0 us)

commit v2 on v0

v2 whole, which is shorter than its diff:
```python
import jax
import jax.numpy as jnp
from jax import lax
from jax.experimental import pallas as pl
from jax.experimental.pallas import tpu as pltpu
from jax.sharding import PartitionSpec as P

MESH = pl.DeviceIdType.MESH
PRECISE = lax.Precision.HIGHEST
V_ROWS = 501
PAD_ROWS = 512
D = 3072
SLICE = 384
COUNT = (32, 48, 48)
START = (0, 32, 80)
STEP = (1, 3)
HALF = ((((0, 16), (16, 16)),) * 2, (((0, 16), (16, 32)), ((0, 32), (32, 16))))
LAUNCH = 2

SCHEDULE = (
    ((0, 0), (
        ("CX",), ("ID",), ("CY",), ("ZG",), ("SZ",), ("CZ", 0, 0, 1), ("CZ", 1, 0, 1), ("S1", 0, 0), ("S1", 0, 1),
        ("LK", 0), ("CZ", 0, 1, 1), ("CZ", 1, 1, 1), ("S1", 1, 0), ("S1", 1, 1), ("LK", 1), ("CZ", 0, 0, 2),
        ("CZ", 1, 0, 2), ("LK", 2), ("S2", 0, 0, 0), ("S2", 0, 1, 0), ("S2", 1, 0, 0), ("S2", 1, 1, 0), ("LK", 3),
        ("LS",), ("CZ", 0, 1, 2), ("CZ", 1, 1, 2), ("F1", 0, 0), ("F1", 0, 1),
    )),
    ((1, 0), (
        ("S2", 0, 0, 3), ("S2", 0, 1, 3), ("CZ", 0, 0, 3), ("CZ", 1, 0, 3), ("CZ", 0, 2, 1), ("CZ", 1, 2, 1),
        ("S2", 0, 0, 1), ("S2", 0, 1, 1), ("S2", 1, 0, 3), ("S2", 1, 1, 3), ("CZ", 0, 1, 3), ("CZ", 1, 1, 3),
        ("F1", 1, 0), ("F1", 1, 1), ("FE",),
    )),
    ((2, 0), (
        ("F2", 0, 0, 0), ("F2", 0, 1, 0), ("CZ", 0, 3, 1), ("CZ", 1, 3, 1), ("S2", 1, 0, 1), ("S2", 1, 1, 1),
        ("CZ", 0, 0, 4), ("CZ", 1, 0, 4),
    )),
    ((0, 3), (
        ("F2", 1, 0, 0), ("F2", 1, 1, 0), ("S2", 0, 0, 2), ("S2", 0, 1, 2),
    )),
    ((0, 1), (
        ("CZ", 0, 2, 2), ("CZ", 1, 2, 2), ("FW",),
    )),
    ((2, 1), (
        ("F2", 0, 0, 3), ("F2", 0, 1, 3), ("CZ", 0, 1, 4), ("CZ", 1, 1, 4), ("F2", 1, 0, 3), ("F2", 1, 1, 3),
    )),
    ((0, 2), (
        ("F2", 0, 0, 1), ("F2", 0, 1, 1), ("CZ", 0, 3, 2), ("CZ", 1, 3, 2), ("F2", 0, 0, 2), ("F2", 0, 1, 2),
    )),
    ((1, 3), (
        ("CZ", 0, 2, 3), ("CZ", 1, 2, 3), ("S2", 1, 0, 2), ("S2", 1, 1, 2),
    )),
    ((1, 1), (
        ("FIN", 0),
    )),
    ((2, 2), (
        ("CZ", 0, 3, 3), ("CZ", 1, 3, 3), ("F2", 1, 0, 1), ("F2", 1, 1, 1), ("CZ", 0, 2, 4), ("CZ", 1, 2, 4),
    )),
    ((1, 2), (
        ("F2", 1, 0, 2), ("F2", 1, 1, 2),
    )),
    ((2, 3), (
        ("CZ", 0, 3, 4), ("CZ", 1, 3, 4),
    )),
)

def logits_of(tokens, rows):
    return lax.dot_general(
        tokens, rows, (((1,), (1,)), ((), ())), preferred_element_type=jnp.float32
    )


def mix(parts):
    peaks = [part[:, 65:66] for part in parts]
    top = peaks[0]
    for peak in peaks[1:]:
        top = jnp.maximum(top, peak)
    total = parts[0] * jnp.exp(peaks[0] - top)
    for part, peak in zip(parts[1:], peaks[1:]):
        total = total + part * jnp.exp(peak - top)
    lane = lax.broadcasted_iota(jnp.int32, total.shape, 1)
    return jnp.where(lane == 65, top, total)


def total_of(parts):
    total = parts[0]
    for part in parts[1:]:
        total = total + part
    return total


def pick(step, values):
    chosen = jnp.int32(values[0])
    for number, value in enumerate(values):
        chosen = jnp.where(step == number, jnp.int32(value), chosen)
    return chosen


def kernel(
    hid_ref, grad_ref, fp_ref, vp_ref, tgt_ref, ids_ref, docs_ref, emb_ref, out_ref,
    hidv, rx, gath, hall_a, hall_bc, emb, pet, idb, part_a, part_bc, part_in_a, part_in_bc,
    look_a, look_bc, look_in_a, look_in_bc, q1_a, q1_bc, q1_in_a, q1_in_bc,
    q2, q2_in, tok, feat, side, sd_in, sz, sz_in, turned,
    sem_l, sem_c, sem_zg, sem_cx, sem_cz, sem_1, sem_2, sem_i, sem_s, sem_r, sem_q, sem_t,
):
    g, v = lax.axis_index("dp"), lax.axis_index("vocab")
    x, y = lax.rem(g, 4), lax.div(g, 4)
    z, c = lax.div(v, 2), lax.rem(v, 2)
    hall = (hall_a, hall_bc.at[0], hall_bc.at[1])
    part = (part_a, part_bc.at[0], part_bc.at[1])
    part_in = (part_in_a, part_in_bc.at[0], part_in_bc.at[1])
    look = (look_a, look_bc.at[0], look_bc.at[1])
    look_in = (look_in_a, look_in_bc.at[0], look_in_bc.at[1])
    q1 = (q1_a, q1_bc.at[0], q1_bc.at[1])
    q1_in = (q1_in_a, q1_in_bc.at[0], q1_in_bc.at[1])

    def dev(dx=0, dy=0, dz=0, dc=0):
        return (
            lax.rem(y + dy, 4) * 4 + lax.rem(x + dx, 4),
            lax.rem(z + dz, 8) * 2 + lax.rem(c + dc, 2),
        )

    def remote(src, dst, sems, at, to):
        send, recv = sems.at[(0, *at)], sems.at[(1, *at)]
        return pltpu.make_async_remote_copy(
            src_ref=src, dst_ref=dst, send_sem=send, recv_sem=recv, device_id=to, device_id_type=MESH
        )

    sent = []

    def go(copy_of, *args):
        copy_of(*args).start()
        sent.append((copy_of, args))

    def columns(zz):
        return pl.ds(pl.multiple_of(lax.rem(zz, 8) * SLICE, 128), SLICE)

    row_at, inner_at = (y, x, y), (x, y, x)

    def inner(cls, k):
        return dev(dy=k) if cls == 1 else dev(dx=k)

    def outer(cls, k):
        return dev(dx=k) if cls == 1 else dev(dy=k)

    emb_local = pltpu.make_async_copy(emb_ref, emb.at[c], sem_l.at[0])
    emb_local.start()
    barrier = pltpu.get_barrier_semaphore()
    peers = [dev(dc=1)] + [dev(dz=k) for k in range(1, 8)]
    peers += [dev(dx=k) for k in range(1, 4)] + [dev(dy=k) for k in range(1, 4)]
    for peer in peers:
        pl.semaphore_signal(barrier, inc=1, device_id=peer, device_id_type=MESH)
    first = c == 0
    hidv[...] = jnp.transpose(hid_ref[...].astype(jnp.float32)).astype(jnp.bfloat16)
    row_id = lax.broadcasted_iota(jnp.int32, (8, 128), 0)
    own_tgt = jnp.where(first, tgt_ref[0:1], tgt_ref[1:2])
    own_ids = jnp.where(first, ids_ref[0:1], ids_ref[1:2])
    idb[y, x] = jnp.where(row_id == 0, own_tgt, own_ids)
    pet[c] = jnp.zeros((128, PAD_ROWS), jnp.bfloat16)
    pet[c, :64, :V_ROWS] = vp_ref[...]
    ones_at = lax.broadcasted_iota(jnp.int32, (16, PAD_ROWS), 0) == 0
    in_table = lax.broadcasted_iota(jnp.int32, (16, PAD_ROWS), 1) < V_ROWS
    pet[c, 64:80] = jnp.where(ones_at & in_table, 1.0, 0.0).astype(jnp.bfloat16)
    pl.semaphore_wait(barrier, len(peers))

    other = pl.multiple_of((1 - c) * 128, 128)
    mine = pl.multiple_of(c * 128, 128)

    def hid_swap():
        return remote(hidv.at[pl.ds(other, 128)], rx, sem_c, (0,), dev(dc=1))

    def pet_swap():
        return remote(pet.at[c], pet.at[c], sem_c, (1,), dev(dc=1))

    def emb_swap():
        return remote(emb_ref, emb.at[c], sem_c, (2,), dev(dc=1))

    def side_swap():
        return remote(side.at[pl.ds(other, 128)], sd_in, sem_c, (3,), dev(dc=1))

    def feat_swap():
        return remote(feat.at[c], feat.at[c], sem_c, (4,), dev(dc=1))

    def tok_swap():
        return remote(tok.at[c], tok.at[c], sem_c, (5,), dev(dc=1))

    def ids_x(k):
        return remote(idb.at[y, x], idb.at[y, x], sem_i, (0, k - 1), dev(dx=k))

    def ids_y(k):
        return remote(idb.at[y], idb.at[y], sem_i, (1, k - 1), dev(dy=k))

    def along_z(k):
        block = gath.at[:, columns(z)]
        return remote(block, block, sem_zg, (k - 1,), dev(dz=k))

    def last_x(k):
        block = hall[2].at[y, x, :, columns(z)]
        return remote(block, block, sem_cx, (0, k - 1), dev(dx=k))

    def last_y(k):
        block = hall[2].at[y, :, :, columns(z)]
        return remote(block, block, sem_cx, (1, k - 1), dev(dy=k))

    def last_z(way, sub, step):
        at = columns(z + 9 - step) if way == 0 else columns(z + step - 1)
        row = lax.rem(y + sub, 4)
        cut = pl.ds(way * 2, 2) if step == 4 else slice(None)
        block = hall[2].at[row, cut, :, at]
        return remote(block, block, sem_cz, (way, sub, step - 1), dev(dz=1 if way == 0 else 7))

    def own_rows(cls):
        return gath.at[pl.ds(START[cls], COUNT[cls])]

    def first_own(cls, way):
        dst = hall[cls].at[row_at[cls], inner_at[cls]]
        return remote(own_rows(cls), dst, sem_1, (cls, way, 0), inner(cls, STEP[way]))

    def first_on(cls, way):
        pos = lax.rem(inner_at[cls] + 4 - STEP[way], 4)
        block = hall[cls].at[row_at[cls], pos, pl.ds(*HALF[cls][0][way])]
        return remote(block, block, sem_1, (cls, way, 1), inner(cls, STEP[way]))

    def second_own(cls, way, k):
        dst = hall[cls].at[row_at[cls], lax.rem(inner_at[cls] + k, 4)]
        src = own_rows(cls) if k == 0 else dst
        return remote(src, dst, sem_2, (cls, way, 0, k), outer(cls, STEP[way]))

    def second_on(cls, way, k):
        row = lax.rem(row_at[cls] + 4 - STEP[way], 4)
        block = hall[cls].at[row, lax.rem(inner_at[cls] + k, 4), pl.ds(*HALF[cls][k % 2][way])]
        return remote(block, block, sem_2, (cls, way, 1, k), outer(cls, STEP[way]))

    def side_z(k):
        to = pl.multiple_of(lax.rem(z + k, 8) * 16, 16)
        return remote(sz.at[pl.ds(to, 16)], sz_in.at[k - 1], sem_s, (0, k - 1), dev(dz=k))

    def feat_z(k):
        return remote(feat.at[c, z], feat.at[c, z], sem_s, (1, k - 1), dev(dz=k))

    def look_out(cls, k):
        return remote(
            look[cls].at[lax.rem(row_at[cls] + k, 4)], look_in[cls].at[k - 1], sem_r, (0, cls, k - 1), outer(cls, k)
        )

    def part_out(cls, k):
        return remote(part[cls].at[k], part_in[cls].at[k - 1], sem_r, (1, cls, k - 1), outer(cls, k))

    def q1_out(cls, k):
        src = q1[cls].at[lax.rem(inner_at[cls] + k, 4)]
        return remote(src, q1_in[cls].at[k - 1], sem_q, (cls, k - 1), inner(cls, k))

    def q2_out(k):
        to = pl.multiple_of(lax.rem(z + k, 8) * 16, 16)
        return remote(q2.at[pl.ds(to, 16)], q2_in.at[k - 1], sem_t, (0, k - 1), dev(dz=k))

    def tok_out(k):
        return remote(tok.at[c, z], tok.at[c, z], sem_t, (1, k - 1), dev(dz=k))

    go(hid_swap)
    for k in (1, 2, 3):
        go(ids_x, k)
    go(pet_swap)
    hid_swap().wait_recv()
    own_half, got_half = hidv[pl.ds(mine, 128), :], rx[...]
    left = jnp.where(first, own_half, got_half)
    right = jnp.where(first, got_half, own_half)
    both = jnp.concatenate([left, right], axis=1)
    hall_bc[1, y, x, :, columns(z)] = both[START[2] :]
    for k in (1, 3, 2):
        go(last_x, k)
    gath[:, columns(z)] = both[: START[2]]
    for k in (1, 7, 2, 6, 3, 5, 4):
        go(along_z, k)
    go(emb_swap)

    side_t = jnp.concatenate(
        [
            jnp.dot(fp_ref[...], hid_ref[...], preferred_element_type=jnp.float32),
            jnp.dot(fp_ref[...], grad_ref[...], preferred_element_type=jnp.float32),
        ],
        axis=0,
    )
    side[...] = jnp.transpose(side_t)
    go(side_swap)

    keep = [
        pltpu.make_async_copy(own_rows(cls), hall[cls].at[row_at[cls], inner_at[cls]], sem_l.at[1 + cls])
        for cls in (0, 1)
    ]
    row_base = (g * 16 + z * 2) * V_ROWS

    def look_up(gy, gx):
        ids = idb[gy, gx]
        wanted = jnp.concatenate([ids[0:1], ids[1:2]], axis=1) - row_base
        found = []
        for b in range(2):
            numbers = lax.broadcasted_iota(jnp.int32, (PAD_ROWS, 256), 0) + b * V_ROWS
            hit = jnp.where(numbers == wanted, 1.0, 0.0).astype(jnp.bfloat16)
            found.append(jnp.dot(pet[b, :64], hit, preferred_element_type=jnp.float32))
        found = total_of(found)
        stacked = jnp.concatenate([found[:, :128], found[:, 128:]], axis=0)
        rows = jnp.transpose(stacked).astype(jnp.bfloat16)
        look_a[gy, gx] = rows[: START[1]]
        look_bc[0, gx, gy] = rows[START[1] : START[2]]
        look_bc[1, gy, gx] = rows[START[2] :]

    arrived = set()

    def handle(what, *at):
        arrived.add((what, *at))
        if what == "CX":
            for k in (1, 2, 3):
                last_x(k).wait_recv()
            for k in (1, 3, 2):
                go(last_y, k)
        elif what == "CY":
            for k in (1, 2, 3):
                last_y(k).wait_recv()
            for sub in (0, 1):
                for way in (0, 1):
                    go(last_z, way, sub, 1)
        elif what == "CZ":
            way, sub, step = at
            last_z(way, sub, step).wait_recv()
            if step < 4:
                go(last_z, way, sub, step + 1)
            if step == LAUNCH and sub < 2:
                go(last_z, way, sub + 2, 1)
        elif what == "ZG":
            for k in range(1, 8):
                along_z(k).wait_recv()
            for cls in (0, 1):
                for way in (0, 1):
                    go(first_own, cls, way)
            for cls in (0, 1):
                for way in (0, 1):
                    go(second_own, cls, way, 0)
            for copy in keep:
                copy.start()
        elif what == "S1":
            cls, way = at
            first_own(cls, way).wait_recv()
            go(first_on, cls, way)
            for to in (0, 1):
                go(second_own, cls, to, 4 - STEP[way])
        elif what == "F1":
            cls, way = at
            first_on(cls, way).wait_recv()
            if ("F1", cls, 1 - way) in arrived:
                for to in (0, 1):
                    go(second_own, cls, to, 2)
        elif what == "S2":
            second_own(*at).wait_recv()
            go(second_on, *at)
        elif what == "F2":
            second_on(*at).wait_recv()
        elif what == "ID":
            for k in (1, 2, 3):
                ids_x(k).wait_recv()
            for k in (1, 2, 3):
                go(ids_y, k)
        elif what == "SZ":
            side_swap().wait_recv()
            sz[...] = side[pl.ds(mine, 128), :] + sd_in[...]
            for k in range(1, 8):
                go(side_z, k)
        elif what == "FE":
            for k in range(1, 8):
                side_z(k).wait_recv()
            own = sz[pl.ds(pl.multiple_of(z * 16, 16), 16), :]
            feat[c, z] = total_of([own] + [sz_in[k] for k in range(7)])
            for k in range(1, 8):
                go(feat_z, k)
        elif what == "FW":
            for k in range(1, 8):
                feat_z(k).wait_recv()
            go(feat_swap)
        elif what == "LK":
            if at[0] == 0:
                pet_swap().wait_recv()
                for k in (1, 2, 3):
                    ids_y(k).wait_recv()

            def one(gx, carry):
                look_up(at[0], gx)
                return carry

            lax.fori_loop(0, 4, one, 0)
        elif what == "LS":
            for cls in (0, 1, 2):
                for k in (1, 2, 3):
                    go(look_out, cls, k)
            emb_local.wait()
            emb_swap().wait_recv()
            for copy in keep:
                copy.wait()
        elif what == "FIN":
            (cls,) = at
            for k in (1, 2, 3):
                part_out(cls, k).wait_recv()
                look_out(cls, k).wait_recv()
            mixed = mix([part[cls][0]] + [part_in[cls][k] for k in range(3)])
            looked = total_of(
                [look[cls][row_at[cls]].astype(jnp.float32)]
                + [look_in[cls][k].astype(jnp.float32) for k in range(3)]
            )
            q1[cls][:, :, :128] = mixed.reshape(4, COUNT[cls], 128)
            q1[cls][:, :, 128:] = looked
            for k in (1, 3, 2):
                go(q1_out, cls, k)

    def partial_sums(tokens):
        logits = [logits_of(tokens, emb[b]) for b in range(2)]
        top = jnp.maximum(*[jnp.max(one, axis=1, keepdims=True) for one in logits])
        pieces = []
        for b in range(2):
            scaled = jnp.exp(logits[b] - top)
            coarse = scaled.astype(jnp.bfloat16)
            fine = (scaled - coarse.astype(jnp.float32)).astype(jnp.bfloat16)
            table = pet[b, :, :V_ROWS]
            pieces += [logits_of(coarse, table), logits_of(fine, table)]
        acc = total_of(pieces)
        lane = lax.broadcasted_iota(jnp.int32, acc.shape, 1)
        return jnp.where(lane == 65, top, acc)

    def tile(step, carry):
        for number, (_, before) in enumerate(SCHEDULE):

            @pl.when(step == number)
            def _(before=before):
                for event in before:
                    handle(*event)

        cls = pick(step, [which[0] for which, _ in SCHEDULE])
        k = pick(step, [which[1] for which, _ in SCHEDULE])

        @pl.when(cls == 0)
        def _():
            part_a[k] = partial_sums(hall_a[lax.rem(y + k, 4)].reshape(4 * COUNT[0], D))

        @pl.when(cls > 0)
        def _():
            at = jnp.where(cls == 1, x, y)
            tokens = hall_bc[cls - 1, lax.rem(at + k, 4)].reshape(4 * COUNT[1], D)
            part_bc[cls - 1, k] = partial_sums(tokens)

        for number, (which, _) in enumerate(SCHEDULE):
            if which[1] > 0:

                @pl.when(step == number)
                def _(which=which):
                    go(part_out, *which)

        return carry

    lax.fori_loop(0, len(SCHEDULE), tile, 0)

    for cls in (0, 1, 2):
        if ("FIN", cls) not in arrived:
            handle("FIN", cls)
    for cls in (0, 1, 2):
        for k in (1, 2, 3):
            q1_out(cls, k).wait_recv()
        own = q1[cls][inner_at[cls]]
        rows = slice(START[cls], START[cls] + COUNT[cls])
        q2[rows, :128] = mix([own[:, :128]] + [q1_in[cls][k, :, :128] for k in range(3)])
        q2[rows, 128:] = total_of([own[:, 128:]] + [q1_in[cls][k, :, 128:] for k in range(3)])
    for k in range(1, 8):
        go(q2_out, k)
    for k in range(1, 8):
        q2_out(k).wait_recv()
    sums = [q2[pl.ds(pl.multiple_of(z * 16, 16), 16), :]] + [q2_in[k] for k in range(7)]
    mixed = mix([one[:, :128] for one in sums])
    looked = total_of([one[:, 128:] for one in sums])
    head = mixed[:, :64] / mixed[:, 64:65] - looked[:, :64]
    tok[c, z] = jnp.concatenate([head, looked[:, 64:]], axis=1)
    for k in range(1, 8):
        go(tok_out, k)
    for k in range(1, 8):
        tok_out(k).wait_recv()
    go(tok_swap)
    feat_swap().wait_recv()
    tok_swap().wait_recv()

    for half in range(2):
        turned[half] = jnp.transpose(tok[half].reshape(128, 128))
    local = jnp.concatenate([docs_ref[0:1], docs_ref[1:2]], axis=1) - g * 4
    feats = feat[...].reshape(256, 128)
    member = [jnp.where(local == d, 1.0, 0.0) for d in range(4)]

    def products(start, right):
        left = jnp.concatenate([turned[half, pl.ds(start, 32, stride=2), :] for half in range(2)], axis=1)
        left = jnp.concatenate([left * m for m in member], axis=0)
        return jnp.dot(left, right, precision=PRECISE, preferred_element_type=jnp.float32)

    even = products(0, feats[:, :64]) + products(64, feats[:, 64:])
    odd = products(1, feats[:, :64]) + products(65, feats[:, 64:])
    result = jnp.concatenate([even, odd], axis=1)
    for d in range(4):
        out_ref[:, d, :] = result[d * 32 : d * 32 + 32]

    for copy_of, args in sent:
        copy_of(*args).wait_send()


def per_device(hidden, input_grad, embedding, vocab_proj, feature_proj, token_ids, targets, doc_ids):
    vmem = pl.BlockSpec(memory_space=pltpu.VMEM)
    bf16, f32, i32 = jnp.bfloat16, jnp.float32, jnp.int32
    dma = pltpu.SemaphoreType.DMA
    na, nb = COUNT[0], COUNT[1]
    out = pl.pallas_call(
        kernel,
        out_shape=jax.ShapeDtypeStruct((32, 4, 128), f32),
        in_specs=[vmem] * 7 + [pl.BlockSpec(memory_space=pl.ANY)],
        out_specs=vmem,
        scratch_shapes=[
            pltpu.VMEM((256, 192), bf16),
            pltpu.VMEM((128, 192), bf16),
            pltpu.VMEM((START[2], D), bf16),
            pltpu.VMEM((4, 4, na, D), bf16),
            pltpu.VMEM((2, 4, 4, nb, D), bf16),
            pltpu.VMEM((2, V_ROWS, D), bf16),
            pltpu.VMEM((2, 128, PAD_ROWS), bf16),
            pltpu.VMEM((4, 4, 8, 128), i32),
            pltpu.VMEM((4, 4 * na, 128), f32),
            pltpu.VMEM((2, 4, 4 * nb, 128), f32),
            pltpu.VMEM((3, 4 * na, 128), f32),
            pltpu.VMEM((2, 3, 4 * nb, 128), f32),
            pltpu.VMEM((4, 4, na, 128), bf16),
            pltpu.VMEM((2, 4, 4, nb, 128), bf16),
            pltpu.VMEM((3, 4, na, 128), bf16),
            pltpu.VMEM((2, 3, 4, nb, 128), bf16),
            pltpu.VMEM((4, na, 256), f32),
            pltpu.VMEM((2, 4, nb, 256), f32),
            pltpu.VMEM((3, na, 256), f32),
            pltpu.VMEM((2, 3, nb, 256), f32),
            pltpu.VMEM((128, 256), f32),
            pltpu.VMEM((7, 16, 256), f32),
            pltpu.VMEM((2, 8, 16, 128), f32),
            pltpu.VMEM((2, 8, 16, 128), f32),
            pltpu.VMEM((256, 128), f32),
            pltpu.VMEM((128, 128), f32),
            pltpu.VMEM((128, 128), f32),
            pltpu.VMEM((7, 16, 128), f32),
            pltpu.VMEM((2, 128, 128), f32),
            dma((3,)),
            dma((2, 6)),
            dma((2, 7)),
            dma((2, 2, 3)),
            dma((2, 2, 4, 4)),
            dma((2, 2, 2, 2)),
            dma((2, 2, 2, 2, 4)),
            dma((2, 2, 3)),
            dma((2, 2, 7)),
            dma((2, 2, 3, 3)),
            dma((2, 3, 3)),
            dma((2, 2, 7)),
        ],
        compiler_params=pltpu.CompilerParams(
            collective_id=0, has_side_effects=True, vmem_limit_bytes=60 * 2**20
        ),
        name="doc_grads",
    )(
        hidden.T, input_grad.T, feature_proj.T, vocab_proj.T,
        targets.reshape(2, 128), token_ids.reshape(2, 128), doc_ids.reshape(2, 128), embedding,
    )
    return out.transpose(1, 0, 2).reshape(4, 4096)


def solution(mesh):
    placed = (
        P("dp", "vocab"),
        P("dp", "vocab"),
        P(("dp", "vocab"), None),
        P(("dp", "vocab"), None),
        P("vocab", None),
        P("dp"),
        P("dp"),
        P("dp"),
    )
    return jax.shard_map(
        per_device, mesh=mesh, in_specs=placed, out_specs=P("dp", None), check_vma=False
    )
```

time: 603 us -> 117 us (0.19)
  waiting for transfers between devices: 357 us -> 0 us
  blocking collectives: 188 us -> 0 us
  Pallas kernels: 0 us -> 115 us
  matrix products: 34.9 us -> 0 us
  between operations: 13.3 us -> 0.01 us
  other arithmetic: 7.6 us -> 0 us
    all_gather x2 -> x0, waiting for transfers between devices: 171 us -> none  [the longest x1 126 us: per_device(): lax.all_gather(full_rows, 'dp', axis=0, tiled=True)]
    pallas_call x0 -> x1, Pallas kernels: none -> 115 us  [per_device(): pl.pallas_call(kernel, out_shape=jax.ShapeDtypeStruct((32, 4, 128), f32),...]
    psum x1 -> x0, waiting for transfers between devices: 112 us -> none  [per_device(): token_side, feature_side = lax.psum((vocab_terms, side_terms), 'vocab')]
    pmax x1 -> x0, blocking collectives: 76.4 us -> none  [per_device(): maximum = lax.pmax(local_peak, ('dp', 'vocab'))]
    psum x1 -> x0, blocking collectives: 74 us -> none  [per_device(): summed_exp = lax.psum(local_total * rescale, ('dp', 'vocab'))]
    reduce_scatter x1 -> x0, waiting for transfers between devices: 72.8 us -> none  [per_device(): lax.psum_scatter(token_terms, 'dp', scatter_dimension=0, tiled=True)]
    all_gather x2 -> x0, blocking collectives: 37.3 us -> none  [the longest x1 19.4 us: per_device(): lax.all_gather(token_ids, 'dp', axis=0, tiled=True)]
    dot_general x7 -> x0, matrix products: 34.9 us -> none  [the longest x1 19.8 us: contract_rows(): lax.dot_general(left_mat, right_mat, (((1,), (1,)), ((), ())), preferred_...]
  transfers between devices with their start and end apart: 4 -> 0, of which waited for: 4 -> 0; matrix products, arithmetic and copies ran while one was open for 1% -> 0% of each run, Pallas kernels for 0% -> 0%
where the time goes in v2:
time: 117 us; the launch traced here: 116 us
  Pallas kernels  115 us (98%)
  local copies, waits for them, and re-layouts  1.47 us (1%)
    pallas_call x1, Pallas kernels, per_device(): pl.pallas_call(kernel, out_shape=jax.ShapeDtypeStruct((32, 4, 128), f32),...  115 us

profile of v2, /device:TPU:1, one launch (start us, length us, event | category | flops | bytes accessed | tf_op | source)
XLA Modules:
  0.0 116.5 jit_solution(1148794075519856294)
XLA Ops:
  0.0 115.0 %doc_grads.1 = f32[32,4,128]{2,1,0:T(4,128)} custom-call(bf16[192,256]{1,0:T(8,128)(2,1)} %bitcast.11, bf16[192,256]{1,0:T(8,128)(2,1)} %bitcast.12, bf16[64,192]{1,0:T(8,128)(2,1)} %bitcast.14, bf16[64,501]{1,0:T(8,128)(2,1)} %bitcast.13, s32[2,128]{1,0:T(2,128)} %bitcast.15, s32[2,128]{1,0:T(2,128)} %bitcast.16, s32[2,128]{1,0:T(2,128)} %bitcast.17, ...), custom_call_target="tpu_custom_call" | custom-call | tf_op jit(solution)/shard_map/doc_grads/pallas_call | solution.py:510
  115.0 1.5 %copy.10 = f32[4,4096]{1,0:T(4,128)} copy(f32[4,4096]{1,0:T(4,128)} %bitcast.10) | data formatting | bytes 131072

commit v3 on v2

--- a/solution.py
+++ b/solution.py
@@ -15,52 +15,51 @@
 START = (0, 32, 80)
 STEP = (1, 3)
 HALF = ((((0, 16), (16, 16)),) * 2, (((0, 16), (16, 32)), ((0, 32), (32, 16))))
-LAUNCH = 2
+LAUNCH = 3
 
 SCHEDULE = (
-    ((0, 0), (
-        ("CX",), ("ID",), ("CY",), ("ZG",), ("SZ",), ("CZ", 0, 0, 1), ("CZ", 1, 0, 1), ("S1", 0, 0), ("S1", 0, 1),
-        ("LK", 0), ("CZ", 0, 1, 1), ("CZ", 1, 1, 1), ("S1", 1, 0), ("S1", 1, 1), ("LK", 1), ("CZ", 0, 0, 2),
-        ("CZ", 1, 0, 2), ("LK", 2), ("S2", 0, 0, 0), ("S2", 0, 1, 0), ("S2", 1, 0, 0), ("S2", 1, 1, 0), ("LK", 3),
-        ("LS",), ("CZ", 0, 1, 2), ("CZ", 1, 1, 2), ("F1", 0, 0), ("F1", 0, 1),
-    )),
-    ((1, 0), (
-        ("S2", 0, 0, 3), ("S2", 0, 1, 3), ("CZ", 0, 0, 3), ("CZ", 1, 0, 3), ("CZ", 0, 2, 1), ("CZ", 1, 2, 1),
-        ("S2", 0, 0, 1), ("S2", 0, 1, 1), ("S2", 1, 0, 3), ("S2", 1, 1, 3), ("CZ", 0, 1, 3), ("CZ", 1, 1, 3),
-        ("F1", 1, 0), ("F1", 1, 1), ("FE",),
-    )),
-    ((2, 0), (
-        ("F2", 0, 0, 0), ("F2", 0, 1, 0), ("CZ", 0, 3, 1), ("CZ", 1, 3, 1), ("S2", 1, 0, 1), ("S2", 1, 1, 1),
-        ("CZ", 0, 0, 4), ("CZ", 1, 0, 4),
-    )),
-    ((0, 3), (
-        ("F2", 1, 0, 0), ("F2", 1, 1, 0), ("S2", 0, 0, 2), ("S2", 0, 1, 2),
-    )),
-    ((0, 1), (
-        ("CZ", 0, 2, 2), ("CZ", 1, 2, 2), ("FW",),
-    )),
-    ((2, 1), (
-        ("F2", 0, 0, 3), ("F2", 0, 1, 3), ("CZ", 0, 1, 4), ("CZ", 1, 1, 4), ("F2", 1, 0, 3), ("F2", 1, 1, 3),
-    )),
-    ((0, 2), (
-        ("F2", 0, 0, 1), ("F2", 0, 1, 1), ("CZ", 0, 3, 2), ("CZ", 1, 3, 2), ("F2", 0, 0, 2), ("F2", 0, 1, 2),
-    )),
-    ((1, 3), (
-        ("CZ", 0, 2, 3), ("CZ", 1, 2, 3), ("S2", 1, 0, 2), ("S2", 1, 1, 2),
-    )),
-    ((1, 1), (
-        ("FIN", 0),
-    )),
-    ((2, 2), (
-        ("CZ", 0, 3, 3), ("CZ", 1, 3, 3), ("F2", 1, 0, 1), ("F2", 1, 1, 1), ("CZ", 0, 2, 4), ("CZ", 1, 2, 4),
-    )),
-    ((1, 2), (
-        ("F2", 1, 0, 2), ("F2", 1, 1, 2),
-    )),
-    ((2, 3), (
-        ("CZ", 0, 3, 4), ("CZ", 1, 3, 4),
+    ((1, (0,)), (
+        ("ZG", 1), ("CX",), ("ID",), ("ZG", 2), ("CZ", 0, 0, 1), ("CZ", 1, 0, 1), ("ZG", 3), ("CY",),
+        ("CZ", 0, 0, 2), ("CZ", 1, 0, 2), ("ZG", 4), ("SZ",), ("CZ", 1, 1, 1), ("S1", 0, 0), ("S1", 0, 1),
+        ("CZ", 0, 1, 1), ("S1", 1, 0), ("S1", 1, 1), ("P2",), ("LK", 0), ("CZ", 1, 0, 3), ("CZ", 0, 0, 3), ("LK", 1),
+        ("S2", 0, 0, 0), ("S2", 0, 1, 0), ("LK", 2), ("CZ", 1, 1, 2), ("S2", 1, 0, 0), ("S2", 1, 1, 0), ("LK", 3),
+        ("LS",), ("CZ", 0, 1, 2), ("F1", 1, 0), ("CZ", 1, 0, 4), ("F1", 1, 1), ("CZ", 0, 0, 4),
+    )),
+    ((0, (0,)), (
+        ("F1", 0, 0), ("F1", 0, 1), ("CZ", 1, 2, 1), ("CZ", 0, 2, 1),
+    )),
+    ((2, (0,)), (
+        ("S2", 0, 0, 3), ("S2", 0, 1, 3), ("CZ", 1, 1, 3), ("CZ", 0, 1, 3), ("S2", 1, 0, 3), ("S2", 1, 1, 3),
+        ("FE",),
+    )),
+    ((2, (1,)), (
+        ("S2", 0, 0, 1), ("S2", 0, 1, 1), ("CZ", 1, 2, 2), ("CZ", 0, 2, 2), ("CZ", 1, 1, 4), ("CZ", 0, 1, 4),
+        ("L1",),
+    )),
+    ((0, (1, 3)), (
+        ("S2", 0, 0, 2), ("S2", 0, 1, 2), ("S2", 1, 0, 1), ("S2", 1, 1, 1), ("CZ", 1, 3, 1), ("CZ", 0, 3, 1),
+        ("F2", 0, 0, 0), ("F2", 0, 1, 0),
+    )),
+    ((1, (1, 3)), (
+        ("F2", 0, 0, 3), ("F2", 0, 1, 3), ("CZ", 1, 2, 3), ("CZ", 0, 2, 3), ("F2", 0, 0, 1), ("F2", 0, 1, 1),
+        ("S2", 1, 0, 2), ("S2", 1, 1, 2),
+    )),
+    ((0, (2,)), (
+        ("CZ", 1, 3, 2), ("CZ", 0, 3, 2), ("F2", 0, 0, 2), ("F2", 0, 1, 2), ("CZ", 1, 2, 4), ("CZ", 0, 2, 4),
+        ("F2", 1, 0, 0), ("F2", 1, 1, 0), ("L2",), ("FIN", 0),
+    )),
+    ((2, (3,)), (
+        ("F2", 1, 0, 3), ("F2", 1, 1, 3), ("FW",), ("FIN", 1),
+    )),
+    ((1, (2,)), (
+        ("F2", 1, 0, 1), ("F2", 1, 1, 1), ("CZ", 1, 3, 3), ("CZ", 0, 3, 3), ("F2", 1, 0, 2), ("F2", 1, 1, 2),
+        ("L3",),
+    )),
+    ((2, (2,)), (
+        ("CZ", 1, 3, 4), ("CZ", 0, 3, 4), ("FIN", 2),
     )),
 )
+
 
 def logits_of(tokens, rows):
     return lax.dot_general(
@@ -97,9 +96,9 @@
 def kernel(
     hid_ref, grad_ref, fp_ref, vp_ref, tgt_ref, ids_ref, docs_ref, emb_ref, out_ref,
     hidv, rx, gath, hall_a, hall_bc, emb, pet, idb, part_a, part_bc, part_in_a, part_in_bc,
-    look_a, look_bc, look_in_a, look_in_bc, q1_a, q1_bc, q1_in_a, q1_in_bc,
-    q2, q2_in, tok, feat, side, sd_in, sz, sz_in, turned,
-    sem_l, sem_c, sem_zg, sem_cx, sem_cz, sem_1, sem_2, sem_i, sem_s, sem_r, sem_q, sem_t,
+    look_a, look_bc, look_in_a, look_in_bc, look_q_a, look_q_bc, look_q_in_a, look_q_in_bc, look_z, look_z_in, found,
+    far_in_a, far_in_bc, q1_a, q1_bc, q1_in_a, q1_in_bc, q2, q2_in, tok, emb_tok, feat, side, sd_in, sz, sz_in, turned,
+    sem_l, sem_c, sem_zg, sem_cx, sem_cz, sem_1, sem_2, sem_i, sem_s, sem_r, sem_f, sem_q, sem_t, sem_h,
 ):
     g, v = lax.axis_index("dp"), lax.axis_index("vocab")
     x, y = lax.rem(g, 4), lax.div(g, 4)
@@ -111,6 +110,9 @@
     look_in = (look_in_a, look_in_bc.at[0], look_in_bc.at[1])
     q1 = (q1_a, q1_bc.at[0], q1_bc.at[1])
     q1_in = (q1_in_a, q1_in_bc.at[0], q1_in_bc.at[1])
+    far_in = (far_in_a, far_in_bc.at[0], far_in_bc.at[1])
+    look_q = (look_q_a, look_q_bc.at[0], look_q_bc.at[1])
+    look_q_in = (look_q_in_a, look_q_in_bc.at[0], look_q_in_bc.at[1])
 
     def dev(dx=0, dy=0, dz=0, dc=0):
         return (
@@ -144,8 +146,9 @@
     emb_local = pltpu.make_async_copy(emb_ref, emb.at[c], sem_l.at[0])
     emb_local.start()
     barrier = pltpu.get_barrier_semaphore()
-    peers = [dev(dc=1)] + [dev(dz=k) for k in range(1, 8)]
+    peers = [dev(dc=1)] + [dev(dz=k, dc=core) for k in range(1, 8) for core in (0, 1)]
     peers += [dev(dx=k) for k in range(1, 4)] + [dev(dy=k) for k in range(1, 4)]
+    peers += [dev(dx=k, dy=2) for k in (1, 2, 3)] + [dev(dx=2, dy=k) for k in (1, 3)]
     for peer in peers:
         pl.semaphore_signal(barrier, inc=1, device_id=peer, device_id_type=MESH)
     first = c == 0
@@ -179,8 +182,8 @@
     def feat_swap():
         return remote(feat.at[c], feat.at[c], sem_c, (4,), dev(dc=1))
 
-    def tok_swap():
-        return remote(tok.at[c], tok.at[c], sem_c, (5,), dev(dc=1))
+    def emb_tok_swap():
+        return remote(emb_tok.at[c], emb_tok.at[c], sem_c, (5,), dev(dc=1))
 
     def ids_x(k):
         return remote(idb.at[y, x], idb.at[y, x], sem_i, (0, k - 1), dev(dx=k))
@@ -188,9 +191,10 @@
     def ids_y(k):
         return remote(idb.at[y], idb.at[y], sem_i, (1, k - 1), dev(dy=k))
 
-    def along_z(k):
-        block = gath.at[:, columns(z)]
-        return remote(block, block, sem_zg, (k - 1,), dev(dz=k))
+    def along_z(way, step):
+        at = columns(z + 9 - step) if way == 0 else columns(z + step - 1)
+        block = gath.at[:, at]
+        return remote(block, block, sem_zg, (way, step - 1), dev(dz=1 if way == 0 else 7))
 
     def last_x(k):
         block = hall[2].at[y, x, :, columns(z)]
@@ -202,7 +206,7 @@
 
     def last_z(way, sub, step):
         at = columns(z + 9 - step) if way == 0 else columns(z + step - 1)
-        row = lax.rem(y + sub, 4)
+        row = lax.rem(y + (0, 1, 3, 2)[sub], 4)
         cut = pl.ds(way * 2, 2) if step == 4 else slice(None)
         block = hall[2].at[row, cut, :, at]
         return remote(block, block, sem_cz, (way, sub, step - 1), dev(dz=1 if way == 0 else 7))
@@ -213,6 +217,16 @@
     def first_own(cls, way):
         dst = hall[cls].at[row_at[cls], inner_at[cls]]
         return remote(own_rows(cls), dst, sem_1, (cls, way, 0), inner(cls, STEP[way]))
+
+    def first_slice(offset):
+        at = columns(z + 8 + offset)
+        for cls in (0, 1):
+            for way in (0, 1):
+                src = gath.at[pl.ds(START[cls], COUNT[cls]), at]
+                dst = hall[cls].at[row_at[cls], inner_at[cls], :, at]
+                remote(src, dst, sem_1, (cls, way, 0), inner(cls, STEP[way])).start()
+                if offset == 0:
+                    sent.append((first_own, (cls, way)))
 
     def first_on(cls, way):
         pos = lax.rem(inner_at[cls] + 4 - STEP[way], 4)
@@ -241,19 +255,35 @@
             look[cls].at[lax.rem(row_at[cls] + k, 4)], look_in[cls].at[k - 1], sem_r, (0, cls, k - 1), outer(cls, k)
         )
 
+    def look_q_out(cls, k):
+        src = look_q[cls].at[lax.rem(inner_at[cls] + k, 4)]
+        return remote(src, look_q_in[cls].at[k - 1], sem_q, (1, cls, k - 1), inner(cls, k))
+
+    def look_z_out(k):
+        to = pl.multiple_of(lax.rem(z + k, 8) * 16, 16)
+        return remote(look_z.at[pl.ds(to, 16)], look_z_in.at[k - 1], sem_s, (2, k - 1), dev(dz=k))
+
     def part_out(cls, k):
-        return remote(part[cls].at[k], part_in[cls].at[k - 1], sem_r, (1, cls, k - 1), outer(cls, k))
+        return remote(part[cls].at[k], part_in[cls].at[k // 2], sem_r, (1, cls, k - 1), outer(cls, k))
+
+    def far_out(cls, j):
+        src = part[cls].at[2, pl.ds(pl.multiple_of(lax.rem(inner_at[cls] + j, 4) * COUNT[cls], 16), COUNT[cls])]
+        to = dev(dx=2, dy=j) if cls == 1 else dev(dx=j, dy=2)
+        return remote(src, far_in[cls].at[j], sem_f, (cls, j), to)
 
     def q1_out(cls, k):
         src = q1[cls].at[lax.rem(inner_at[cls] + k, 4)]
-        return remote(src, q1_in[cls].at[k - 1], sem_q, (cls, k - 1), inner(cls, k))
+        return remote(src, q1_in[cls].at[k - 1], sem_q, (0, cls, k - 1), inner(cls, k))
 
     def q2_out(k):
         to = pl.multiple_of(lax.rem(z + k, 8) * 16, 16)
         return remote(q2.at[pl.ds(to, 16)], q2_in.at[k - 1], sem_t, (0, k - 1), dev(dz=k))
 
-    def tok_out(k):
-        return remote(tok.at[c, z], tok.at[c, z], sem_t, (1, k - 1), dev(dz=k))
+    def emb_tok_out(k):
+        return remote(emb_tok.at[c, z], emb_tok.at[c, z], sem_t, (1, k - 1), dev(dz=k))
+
+    def tok_out(k, core):
+        return remote(tok.at[c, z], tok.at[c, z], sem_h, (core, k), dev(dz=k, dc=core))
 
     go(hid_swap)
     for k in (1, 2, 3):
@@ -268,8 +298,9 @@
     for k in (1, 3, 2):
         go(last_x, k)
     gath[:, columns(z)] = both[: START[2]]
-    for k in (1, 7, 2, 6, 3, 5, 4):
-        go(along_z, k)
+    for way in (0, 1):
+        go(along_z, way, 1)
+    first_slice(0)
     go(emb_swap)
 
     side_t = jnp.concatenate(
@@ -291,13 +322,13 @@
     def look_up(gy, gx):
         ids = idb[gy, gx]
         wanted = jnp.concatenate([ids[0:1], ids[1:2]], axis=1) - row_base
-        found = []
+        terms = []
         for b in range(2):
             numbers = lax.broadcasted_iota(jnp.int32, (PAD_ROWS, 256), 0) + b * V_ROWS
             hit = jnp.where(numbers == wanted, 1.0, 0.0).astype(jnp.bfloat16)
-            found.append(jnp.dot(pet[b, :64], hit, preferred_element_type=jnp.float32))
-        found = total_of(found)
-        stacked = jnp.concatenate([found[:, :128], found[:, 128:]], axis=0)
+            terms.append(jnp.dot(pet[b, :64], hit, preferred_element_type=jnp.float32))
+        term = total_of(terms)
+        stacked = jnp.concatenate([term[:, :128], term[:, 128:]], axis=0)
         rows = jnp.transpose(stacked).astype(jnp.bfloat16)
         look_a[gy, gx] = rows[: START[1]]
         look_bc[0, gx, gy] = rows[START[1] : START[2]]
@@ -312,12 +343,13 @@
                 last_x(k).wait_recv()
             for k in (1, 3, 2):
                 go(last_y, k)
+            for way in (0, 1):
+                go(last_z, way, 0, 1)
         elif what == "CY":
             for k in (1, 2, 3):
                 last_y(k).wait_recv()
-            for sub in (0, 1):
-                for way in (0, 1):
-                    go(last_z, way, sub, 1)
+            for way in (0, 1):
+                go(last_z, way, 1, 1)
         elif what == "CZ":
             way, sub, step = at
             last_z(way, sub, step).wait_recv()
@@ -326,22 +358,30 @@
             if step == LAUNCH and sub < 2:
                 go(last_z, way, sub + 2, 1)
         elif what == "ZG":
-            for k in range(1, 8):
-                along_z(k).wait_recv()
-            for cls in (0, 1):
-                for way in (0, 1):
-                    go(first_own, cls, way)
-            for cls in (0, 1):
-                for way in (0, 1):
-                    go(second_own, cls, way, 0)
-            for copy in keep:
-                copy.start()
+            (step,) = at
+            for way in (0, 1):
+                if step < 4 or way == 0:
+                    along_z(way, step).wait_recv()
+                if step < 3 or (step == 3 and way == 0):
+                    go(along_z, way, step + 1)
+            first_slice(-step)
+            if step < 4:
+                first_slice(step)
+            else:
+                for cls in (0, 1):
+                    for way in (0, 1):
+                        go(second_own, cls, way, 0)
+                for copy in keep:
+                    copy.start()
         elif what == "S1":
             cls, way = at
             first_own(cls, way).wait_recv()
             go(first_on, cls, way)
-            for to in (0, 1):
-                go(second_own, cls, to, 4 - STEP[way])
+        elif what == "P2":
+            for k in (3, 1):
+                for cls in (0, 1):
+                    for way in (0, 1):
+                        go(second_own, cls, way, k)
         elif what == "F1":
             cls, way = at
             first_on(cls, way).wait_recv()
@@ -393,34 +433,56 @@
             emb_swap().wait_recv()
             for copy in keep:
                 copy.wait()
+        elif what == "L1":
+            for cls in (0, 1, 2):
+                for k in (1, 2, 3):
+                    look_out(cls, k).wait_recv()
+                own = look[cls][row_at[cls]]
+                look_q[cls][...] = total_of([own] + [look_in[cls][k] for k in range(3)])
+                for k in (1, 2, 3):
+                    go(look_q_out, cls, k)
+        elif what == "L2":
+            for cls in (0, 1, 2):
+                for k in (1, 2, 3):
+                    look_q_out(cls, k).wait_recv()
+                own = look_q[cls][inner_at[cls]]
+                look_z[START[cls] : START[cls] + COUNT[cls]] = total_of([own] + [look_q_in[cls][k] for k in range(3)])
+            for k in range(1, 8):
+                go(look_z_out, k)
+        elif what == "L3":
+            for k in range(1, 8):
+                look_z_out(k).wait_recv()
+            own = look_z[pl.ds(pl.multiple_of(z * 16, 16), 16), :]
+            found[...] = total_of([one.astype(jnp.float32) for one in [own] + [look_z_in[k] for k in range(7)]])
+            emb_tok[c, z] = found[...]
+            for k in range(1, 8):
+                go(emb_tok_out, k)
+        elif what == "L4":
+            for k in range(1, 8):
+                emb_tok_out(k).wait_recv()
+            go(emb_tok_swap)
         elif what == "FIN":
             (cls,) = at
-            for k in (1, 2, 3):
+            for k in (1, 3):
                 part_out(cls, k).wait_recv()
-                look_out(cls, k).wait_recv()
-            mixed = mix([part[cls][0]] + [part_in[cls][k] for k in range(3)])
-            looked = total_of(
-                [look[cls][row_at[cls]].astype(jnp.float32)]
-                + [look_in[cls][k].astype(jnp.float32) for k in range(3)]
-            )
-            q1[cls][:, :, :128] = mixed.reshape(4, COUNT[cls], 128)
-            q1[cls][:, :, 128:] = looked
+            q1[cls][...] = mix([part[cls][0], part_in[cls][0], part_in[cls][1]]).reshape(4, COUNT[cls], 128)
             for k in (1, 3, 2):
                 go(q1_out, cls, k)
 
     def partial_sums(tokens):
-        logits = [logits_of(tokens, emb[b]) for b in range(2)]
-        top = jnp.maximum(*[jnp.max(one, axis=1, keepdims=True) for one in logits])
+        logits = [logits_of(emb[b], tokens) for b in range(2)]
+        top = jnp.maximum(*[jnp.max(one, axis=0, keepdims=True) for one in logits])
         pieces = []
         for b in range(2):
             scaled = jnp.exp(logits[b] - top)
             coarse = scaled.astype(jnp.bfloat16)
             fine = (scaled - coarse.astype(jnp.float32)).astype(jnp.bfloat16)
             table = pet[b, :, :V_ROWS]
-            pieces += [logits_of(coarse, table), logits_of(fine, table)]
+            for piece in (coarse, fine):
+                pieces.append(jnp.dot(table, piece, preferred_element_type=jnp.float32))
         acc = total_of(pieces)
-        lane = lax.broadcasted_iota(jnp.int32, acc.shape, 1)
-        return jnp.where(lane == 65, top, acc)
+        row = lax.broadcasted_iota(jnp.int32, acc.shape, 0)
+        return jnp.transpose(jnp.where(row == 65, top, acc))
 
     def tile(step, carry):
         for number, (_, before) in enumerate(SCHEDULE):
@@ -431,24 +493,44 @@
                     handle(*event)
 
         cls = pick(step, [which[0] for which, _ in SCHEDULE])
-        k = pick(step, [which[1] for which, _ in SCHEDULE])
-
-        @pl.when(cls == 0)
+        k = pick(step, [which[1][0] for which, _ in SCHEDULE])
+        pair = pick(step, [len(which[1]) - 1 for which, _ in SCHEDULE])
+        at = jnp.where(cls == 1, x, y)
+
+        @pl.when((cls == 0) & (pair == 0))
         def _():
             part_a[k] = partial_sums(hall_a[lax.rem(y + k, 4)].reshape(4 * COUNT[0], D))
 
-        @pl.when(cls > 0)
+        @pl.when((cls > 0) & (pair == 0))
         def _():
-            at = jnp.where(cls == 1, x, y)
             tokens = hall_bc[cls - 1, lax.rem(at + k, 4)].reshape(4 * COUNT[1], D)
             part_bc[cls - 1, k] = partial_sums(tokens)
 
+        @pl.when((cls > 0) & (pair == 1))
+        def _():
+            rows = [hall_bc[0, lax.rem(x + near, 4)].reshape(4 * COUNT[1], D) for near in (1, 3)]
+            sums = partial_sums(jnp.concatenate(rows, axis=0))
+            part_bc[0, 1] = sums[: 4 * COUNT[1]]
+            part_bc[0, 3] = sums[4 * COUNT[1] :]
+
+        @pl.when((cls == 0) & (pair == 1))
+        def _():
+            rows = [hall_a[lax.rem(y + near, 4)].reshape(4 * COUNT[0], D) for near in (1, 3)]
+            sums = partial_sums(jnp.concatenate(rows, axis=0))
+            part_a[1] = sums[: 4 * COUNT[0]]
+            part_a[3] = sums[4 * COUNT[0] :]
+
         for number, (which, _) in enumerate(SCHEDULE):
-            if which[1] > 0:
+            if which[1] != (0,):
 
                 @pl.when(step == number)
                 def _(which=which):
-                    go(part_out, *which)
+                    for one in which[1]:
+                        if one == 2:
+                            for j in (2, 1, 3, 0):
+                                go(far_out, which[0], j)
+                        else:
+                            go(part_out, which[0], one)
 
         return carry
 
@@ -457,34 +539,30 @@
     for cls in (0, 1, 2):
         if ("FIN", cls) not in arrived:
             handle("FIN", cls)
+    if ("L3",) not in arrived:
+        handle("L3")
     for cls in (0, 1, 2):
         for k in (1, 2, 3):
             q1_out(cls, k).wait_recv()
-        own = q1[cls][inner_at[cls]]
-        rows = slice(START[cls], START[cls] + COUNT[cls])
-        q2[rows, :128] = mix([own[:, :128]] + [q1_in[cls][k, :, :128] for k in range(3)])
-        q2[rows, 128:] = total_of([own[:, 128:]] + [q1_in[cls][k, :, 128:] for k in range(3)])
-    for k in range(1, 8):
+        for j in range(4):
+            far_out(cls, j).wait_recv()
+        parts = [q1[cls][inner_at[cls]]] + [q1_in[cls][k] for k in range(3)] + [far_in[cls][j] for j in range(4)]
+        q2[START[cls] : START[cls] + COUNT[cls]] = mix(parts)
+    for k in (4, 3, 5, 2, 6, 1, 7):
         go(q2_out, k)
+    handle("L4")
     for k in range(1, 8):
         q2_out(k).wait_recv()
-    sums = [q2[pl.ds(pl.multiple_of(z * 16, 16), 16), :]] + [q2_in[k] for k in range(7)]
-    mixed = mix([one[:, :128] for one in sums])
-    looked = total_of([one[:, 128:] for one in sums])
-    head = mixed[:, :64] / mixed[:, 64:65] - looked[:, :64]
-    tok[c, z] = jnp.concatenate([head, looked[:, 64:]], axis=1)
-    for k in range(1, 8):
-        go(tok_out, k)
-    for k in range(1, 8):
-        tok_out(k).wait_recv()
-    go(tok_swap)
+    mixed = mix([q2[pl.ds(pl.multiple_of(z * 16, 16), 16), :]] + [q2_in[k] for k in range(7)])
+    head = mixed[:, :64] / mixed[:, 64:65] - found[:, :64]
+    tok[c, z] = jnp.concatenate([head[:8], head[8:]], axis=1)
+    others = [(k, core) for k in (4, 3, 5, 2, 6, 1, 7, 0) for core in (0, 1) if (k, core) != (0, 0)]
+    for k, core in others:
+        go(tok_out, k, core)
     feat_swap().wait_recv()
-    tok_swap().wait_recv()
-
-    for half in range(2):
-        turned[half] = jnp.transpose(tok[half].reshape(128, 128))
+    emb_tok_swap().wait_recv()
+    feats = feat[...].reshape(256, 128)
     local = jnp.concatenate([docs_ref[0:1], docs_ref[1:2]], axis=1) - g * 4
-    feats = feat[...].reshape(256, 128)
     member = [jnp.where(local == d, 1.0, 0.0) for d in range(4)]
 
     def products(start, right):
@@ -492,8 +570,19 @@
         left = jnp.concatenate([left * m for m in member], axis=0)
         return jnp.dot(left, right, precision=PRECISE, preferred_element_type=jnp.float32)
 
-    even = products(0, feats[:, :64]) + products(64, feats[:, 64:])
-    odd = products(1, feats[:, :64]) + products(65, feats[:, 64:])
+    for half in range(2):
+        turned[half] = jnp.transpose(emb_tok[half].reshape(128, 128))
+    even = products(64, feats[:, 64:])
+    odd = products(65, feats[:, 64:])
+    for k, core in others:
+        tok_out(k, core).wait_recv()
+
+    for half in range(2):
+        rows = [tok[half, :, :, 64 * side : 64 * side + 64].reshape(8, 1, 8, 64) for side in range(2)]
+        heads = jnp.concatenate(rows, axis=1).reshape(128, 64)
+        turned[half, :64] = jnp.transpose(heads)
+    even = even + products(0, feats[:, :64])
+    odd = odd + products(1, feats[:, :64])
     result = jnp.concatenate([even, odd], axis=1)
     for d in range(4):
         out_ref[:, d, :] = result[d * 32 : d * 32 + 32]
@@ -523,18 +612,28 @@
             pltpu.VMEM((4, 4, 8, 128), i32),
             pltpu.VMEM((4, 4 * na, 128), f32),
             pltpu.VMEM((2, 4, 4 * nb, 128), f32),
-            pltpu.VMEM((3, 4 * na, 128), f32),
-            pltpu.VMEM((2, 3, 4 * nb, 128), f32),
+            pltpu.VMEM((2, 4 * na, 128), f32),
+            pltpu.VMEM((2, 2, 4 * nb, 128), f32),
             pltpu.VMEM((4, 4, na, 128), bf16),
             pltpu.VMEM((2, 4, 4, nb, 128), bf16),
             pltpu.VMEM((3, 4, na, 128), bf16),
             pltpu.VMEM((2, 3, 4, nb, 128), bf16),
-            pltpu.VMEM((4, na, 256), f32),
-            pltpu.VMEM((2, 4, nb, 256), f32),
-            pltpu.VMEM((3, na, 256), f32),
-            pltpu.VMEM((2, 3, nb, 256), f32),
-            pltpu.VMEM((128, 256), f32),
-            pltpu.VMEM((7, 16, 256), f32),
+            pltpu.VMEM((4, na, 128), bf16),
+            pltpu.VMEM((2, 4, nb, 128), bf16),
+            pltpu.VMEM((3, na, 128), bf16),
+            pltpu.VMEM((2, 3, nb, 128), bf16),
+            pltpu.VMEM((128, 128), bf16),
+            pltpu.VMEM((7, 16, 128), bf16),
+            pltpu.VMEM((16, 128), f32),
+            pltpu.VMEM((4, na, 128), f32),
+            pltpu.VMEM((2, 4, nb, 128), f32),
+            pltpu.VMEM((4, na, 128), f32),
+            pltpu.VMEM((2, 4, nb, 128), f32),
+            pltpu.VMEM((3, na, 128), f32),
+            pltpu.VMEM((2, 3, nb, 128), f32),
+            pltpu.VMEM((128, 128), f32),
+            pltpu.VMEM((7, 16, 128), f32),
+            pltpu.VMEM((2, 8, 8, 128), f32),
             pltpu.VMEM((2, 8, 16, 128), f32),
             pltpu.VMEM((2, 8, 16, 128), f32),
             pltpu.VMEM((256, 128), f32),
@@ -544,16 +643,18 @@
             pltpu.VMEM((2, 128, 128), f32),
             dma((3,)),
             dma((2, 6)),
-            dma((2, 7)),
+            dma((2, 2, 4)),
             dma((2, 2, 3)),
             dma((2, 2, 4, 4)),
             dma((2, 2, 2, 2)),
             dma((2, 2, 2, 2, 4)),
             dma((2, 2, 3)),
+            dma((2, 3, 7)),
+            dma((2, 2, 3, 3)),
+            dma((2, 3, 4)),
+            dma((2, 2, 3, 3)),
             dma((2, 2, 7)),
-            dma((2, 2, 3, 3)),
-            dma((2, 3, 3)),
-            dma((2, 2, 7)),
+            dma((2, 2, 8)),
         ],
         compiler_params=pltpu.CompilerParams(
             collective_id=0, has_side_effects=True, vmem_limit_bytes=60 * 2**20

time: 117 us -> 108 us (0.923)
  Pallas kernels: 115 us -> 106 us
    pallas_call x1, Pallas kernels: 115 us -> 106 us  [per_device(): pl.pallas_call(kernel, out_shape=jax.ShapeDtypeStruct((32, 4, 128), f32),...]
where the time goes in v3:
time: 108 us
  Pallas kernels  106 us (98%)
  local copies, waits for them, and re-layouts  1.47 us (1%)
    pallas_call x1, Pallas kernels, per_device(): pl.pallas_call(kernel, out_shape=jax.ShapeDtypeStruct((32, 4, 128), f32),...  106 us

profile of v3, /device:TPU:1, one launch (start us, length us, event | category | flops | bytes accessed | tf_op | source)
XLA Modules:
  0.0 107.8 jit_solution(3713471113434652113)
XLA Ops:
  0.0 106.3 %doc_grads.1 = f32[32,4,128]{2,1,0:T(4,128)} custom-call(bf16[192,256]{1,0:T(8,128)(2,1)} %bitcast.11, bf16[192,256]{1,0:T(8,128)(2,1)} %bitcast.12, bf16[64,192]{1,0:T(8,128)(2,1)} %bitcast.14, bf16[64,501]{1,0:T(8,128)(2,1)} %bitcast.13, s32[2,128]{1,0:T(2,128)} %bitcast.15, s32[2,128]{1,0:T(2,128)} %bitcast.16, s32[2,128]{1,0:T(2,128)} %bitcast.17, ...), custom_call_target="tpu_custom_call" | custom-call | tf_op jit(solution)/shard_map/doc_grads/pallas_call | solution.py:599
  106.3 1.5 %copy.10 = f32[4,4096]{1,0:T(4,128)} copy(f32[4,4096]{1,0:T(4,128)} %bitcast.10) | data formatting | bytes 131072

commit v4 on v3

--- a/solution.py
+++ b/solution.py
@@ -15,48 +15,41 @@
 START = (0, 32, 80)
 STEP = (1, 3)
 HALF = ((((0, 16), (16, 16)),) * 2, (((0, 16), (16, 32)), ((0, 32), (32, 16))))
-LAUNCH = 3
+LAUNCH = 2
 
 SCHEDULE = (
-    ((1, (0,)), (
-        ("ZG", 1), ("CX",), ("ID",), ("ZG", 2), ("CZ", 0, 0, 1), ("CZ", 1, 0, 1), ("ZG", 3), ("CY",),
-        ("CZ", 0, 0, 2), ("CZ", 1, 0, 2), ("ZG", 4), ("SZ",), ("CZ", 1, 1, 1), ("S1", 0, 0), ("S1", 0, 1),
-        ("CZ", 0, 1, 1), ("S1", 1, 0), ("S1", 1, 1), ("P2",), ("LK", 0), ("CZ", 1, 0, 3), ("CZ", 0, 0, 3), ("LK", 1),
-        ("S2", 0, 0, 0), ("S2", 0, 1, 0), ("LK", 2), ("CZ", 1, 1, 2), ("S2", 1, 0, 0), ("S2", 1, 1, 0), ("LK", 3),
-        ("LS",), ("CZ", 0, 1, 2), ("F1", 1, 0), ("CZ", 1, 0, 4), ("F1", 1, 1), ("CZ", 0, 0, 4),
-    )),
-    ((0, (0,)), (
-        ("F1", 0, 0), ("F1", 0, 1), ("CZ", 1, 2, 1), ("CZ", 0, 2, 1),
-    )),
-    ((2, (0,)), (
-        ("S2", 0, 0, 3), ("S2", 0, 1, 3), ("CZ", 1, 1, 3), ("CZ", 0, 1, 3), ("S2", 1, 0, 3), ("S2", 1, 1, 3),
-        ("FE",),
-    )),
-    ((2, (1,)), (
-        ("S2", 0, 0, 1), ("S2", 0, 1, 1), ("CZ", 1, 2, 2), ("CZ", 0, 2, 2), ("CZ", 1, 1, 4), ("CZ", 0, 1, 4),
-        ("L1",),
-    )),
-    ((0, (1, 3)), (
-        ("S2", 0, 0, 2), ("S2", 0, 1, 2), ("S2", 1, 0, 1), ("S2", 1, 1, 1), ("CZ", 1, 3, 1), ("CZ", 0, 3, 1),
-        ("F2", 0, 0, 0), ("F2", 0, 1, 0),
-    )),
-    ((1, (1, 3)), (
-        ("F2", 0, 0, 3), ("F2", 0, 1, 3), ("CZ", 1, 2, 3), ("CZ", 0, 2, 3), ("F2", 0, 0, 1), ("F2", 0, 1, 1),
-        ("S2", 1, 0, 2), ("S2", 1, 1, 2),
-    )),
-    ((0, (2,)), (
-        ("CZ", 1, 3, 2), ("CZ", 0, 3, 2), ("F2", 0, 0, 2), ("F2", 0, 1, 2), ("CZ", 1, 2, 4), ("CZ", 0, 2, 4),
-        ("F2", 1, 0, 0), ("F2", 1, 1, 0), ("L2",), ("FIN", 0),
-    )),
-    ((2, (3,)), (
-        ("F2", 1, 0, 3), ("F2", 1, 1, 3), ("FW",), ("FIN", 1),
-    )),
-    ((1, (2,)), (
-        ("F2", 1, 0, 1), ("F2", 1, 1, 1), ("CZ", 1, 3, 3), ("CZ", 0, 3, 3), ("F2", 1, 0, 2), ("F2", 1, 1, 2),
-        ("L3",),
-    )),
-    ((2, (2,)), (
-        ("CZ", 1, 3, 4), ("CZ", 0, 3, 4), ("FIN", 2),
+    ((1, 0, 0, 0), (
+        ("ZG", 1), ("CX",), ("ID",), ("ZG", 2), ("CZ", 0, 0, 1), ("CZ", 1, 0, 1), ("ZG", 3), ("CY", 2), ("CY", 1),
+        ("CY", 3), ("CZ", 0, 0, 2), ("CZ", 1, 0, 2), ("ZG", 4), ("SZ",), ("CZ", 1, 1, 1), ("S1", 0, 0), ("S1", 0, 1),
+        ("CZ", 0, 1, 1), ("S2", 1, 0, 0), ("S2", 1, 1, 0), ("S1", 1, 0), ("S1", 1, 1), ("P2",), ("LK", 0),
+        ("S2", 0, 0, 0), ("LK", 1), ("S2", 0, 1, 0), ("LK", 2), ("CZ", 1, 0, 3), ("CZ", 0, 0, 3), ("F1", 0, 0),
+        ("LK", 3), ("LS",), ("F1", 0, 1), ("CZ", 1, 2, 1), ("CZ", 0, 2, 1), ("F1", 1, 0), ("F1", 1, 1),
+    )),
+    ((2, 0, 0, 1), (
+        ("F2", 1, 0, 0), ("F2", 1, 1, 0), ("CZ", 1, 1, 2), ("CZ", 0, 1, 2), ("CZ", 1, 0, 4), ("S2", 0, 0, 3),
+        ("S2", 0, 1, 3), ("CZ", 0, 0, 4),
+    )),
+    ((2, 1, 1, 0), (
+        ("CZ", 1, 2, 2), ("S2", 1, 0, 3), ("S2", 1, 1, 3), ("CZ", 0, 2, 2), ("S2", 0, 0, 1), ("S2", 0, 1, 1),
+        ("CZ", 1, 1, 3), ("F2", 0, 0, 0), ("F2", 0, 1, 0), ("CZ", 0, 1, 3), ("CZ", 1, 3, 1), ("S2", 1, 0, 1),
+        ("S2", 1, 1, 1), ("CZ", 0, 3, 1), ("S2", 0, 0, 2), ("S2", 0, 1, 2), ("CZ", 1, 2, 3), ("F2", 0, 0, 3),
+        ("F2", 0, 1, 3), ("CZ", 0, 2, 3), ("CZ", 1, 1, 4), ("CZ", 0, 1, 4), ("F2", 0, 0, 1),
+    )),
+    ((1, 1, 1, 1), (
+        ("F2", 0, 1, 1), ("S2", 1, 0, 2), ("S2", 1, 1, 2), ("CZ", 1, 3, 2), ("F2", 0, 0, 2), ("F2", 0, 1, 2),
+        ("CZ", 0, 3, 2),
+    )),
+    ((1, 3, 3, 0), (
+        ("CZ", 1, 2, 4), ("F2", 1, 0, 3), ("F2", 1, 1, 3), ("CZ", 0, 2, 4), ("FE",),
+    )),
+    ((2, 3, 3, 1), (
+        ("F2", 1, 0, 1), ("F2", 1, 1, 1), ("CZ", 1, 3, 3), ("CZ", 0, 3, 3), ("L1",),
+    )),
+    ((1, 2, 2, 0), (
+        ("F2", 1, 0, 2), ("F2", 1, 1, 2),
+    )),
+    ((2, 2, 2, 1), (
+        ("CZ", 1, 3, 4), ("CZ", 0, 3, 4), ("L2",), ("FW",), ("FIN", 1),
     )),
 )
 
@@ -225,8 +218,10 @@
                 src = gath.at[pl.ds(START[cls], COUNT[cls]), at]
                 dst = hall[cls].at[row_at[cls], inner_at[cls], :, at]
                 remote(src, dst, sem_1, (cls, way, 0), inner(cls, STEP[way])).start()
+                remote(src, dst, sem_2, (cls, way, 0, 0), outer(cls, STEP[way])).start()
                 if offset == 0:
                     sent.append((first_own, (cls, way)))
+                    sent.append((second_own, (cls, way, 0)))
 
     def first_on(cls, way):
         pos = lax.rem(inner_at[cls] + 4 - STEP[way], 4)
@@ -334,22 +329,23 @@
         look_bc[0, gx, gy] = rows[START[1] : START[2]]
         look_bc[1, gy, gx] = rows[START[2] :]
 
-    arrived = set()
+    arrived, held = set(), {}
 
     def handle(what, *at):
         arrived.add((what, *at))
         if what == "CX":
             for k in (1, 2, 3):
                 last_x(k).wait_recv()
-            for k in (1, 3, 2):
+            for k in (3, 1, 2):
                 go(last_y, k)
             for way in (0, 1):
                 go(last_z, way, 0, 1)
         elif what == "CY":
-            for k in (1, 2, 3):
-                last_y(k).wait_recv()
-            for way in (0, 1):
-                go(last_z, way, 1, 1)
+            (sub,) = at
+            last_y(4 - (0, 1, 3, 2)[sub]).wait_recv()
+            if sub == 1:
+                for way in (0, 1):
+                    go(last_z, way, 1, 1)
         elif what == "CZ":
             way, sub, step = at
             last_z(way, sub, step).wait_recv()
@@ -368,9 +364,6 @@
             if step < 4:
                 first_slice(step)
             else:
-                for cls in (0, 1):
-                    for way in (0, 1):
-                        go(second_own, cls, way, 0)
                 for copy in keep:
                     copy.start()
         elif what == "S1":
@@ -388,9 +381,14 @@
             if ("F1", cls, 1 - way) in arrived:
                 for to in (0, 1):
                     go(second_own, cls, to, 2)
+                for block in held.pop(cls, ()):
+                    go(second_on, *block)
         elif what == "S2":
             second_own(*at).wait_recv()
-            go(second_on, *at)
+            if True:
+                go(second_on, *at)
+            else:
+                held.setdefault(at[0], []).append(at)
         elif what == "F2":
             second_on(*at).wait_recv()
         elif what == "ID":
@@ -492,45 +490,27 @@
                 for event in before:
                     handle(*event)
 
-        cls = pick(step, [which[0] for which, _ in SCHEDULE])
-        k = pick(step, [which[1][0] for which, _ in SCHEDULE])
-        pair = pick(step, [len(which[1]) - 1 for which, _ in SCHEDULE])
-        at = jnp.where(cls == 1, x, y)
-
-        @pl.when((cls == 0) & (pair == 0))
-        def _():
-            part_a[k] = partial_sums(hall_a[lax.rem(y + k, 4)].reshape(4 * COUNT[0], D))
-
-        @pl.when((cls > 0) & (pair == 0))
-        def _():
-            tokens = hall_bc[cls - 1, lax.rem(at + k, 4)].reshape(4 * COUNT[1], D)
-            part_bc[cls - 1, k] = partial_sums(tokens)
-
-        @pl.when((cls > 0) & (pair == 1))
-        def _():
-            rows = [hall_bc[0, lax.rem(x + near, 4)].reshape(4 * COUNT[1], D) for near in (1, 3)]
-            sums = partial_sums(jnp.concatenate(rows, axis=0))
-            part_bc[0, 1] = sums[: 4 * COUNT[1]]
-            part_bc[0, 3] = sums[4 * COUNT[1] :]
-
-        @pl.when((cls == 0) & (pair == 1))
-        def _():
-            rows = [hall_a[lax.rem(y + near, 4)].reshape(4 * COUNT[0], D) for near in (1, 3)]
-            sums = partial_sums(jnp.concatenate(rows, axis=0))
-            part_a[1] = sums[: 4 * COUNT[0]]
-            part_a[3] = sums[4 * COUNT[0] :]
+        cls, k, near, half = [pick(step, [which[n] for which, _ in SCHEDULE]) for n in range(4)]
+        row = lax.rem(jnp.where(cls == 1, x, y) + k, 4)
+        tokens = hall_bc[cls - 1, row].reshape(4 * COUNT[1], D)
+        beside = hall_a[lax.rem(y + near, 4), pl.ds(half * 2, 2)].reshape(2 * COUNT[0], D)
+        sums = partial_sums(jnp.concatenate([tokens, beside], axis=0))
+        part_bc[cls - 1, k] = sums[: 4 * COUNT[1]]
+        at = pl.multiple_of(half * 2 * COUNT[0], 2 * COUNT[0])
+        part_a[near, pl.ds(at, 2 * COUNT[0])] = sums[4 * COUNT[1] :]
 
         for number, (which, _) in enumerate(SCHEDULE):
-            if which[1] != (0,):
-
-                @pl.when(step == number)
-                def _(which=which):
-                    for one in which[1]:
-                        if one == 2:
-                            for j in (2, 1, 3, 0):
-                                go(far_out, which[0], j)
-                        else:
-                            go(part_out, which[0], one)
+
+            @pl.when(step == number)
+            def _(which=which):
+                for one, turn in ((which[0], which[1]), (0, which[2])):
+                    if one == 0 and which[3] == 0:
+                        continue
+                    if turn == 2:
+                        for j in (2, 1, 3, 0):
+                            go(far_out, one, j)
+                    elif turn > 0:
+                        go(part_out, one, turn)
 
         return carry
 

time: 108 us -> 103 us (0.954)
  Pallas kernels: 106 us -> 101 us
    pallas_call x1, Pallas kernels: 106 us -> 101 us  [per_device(): pl.pallas_call(kernel, out_shape=jax.ShapeDtypeStruct((32, 4, 128), f32),...]
where the time goes in v4:
time: 103 us
  Pallas kernels  101 us (98%)
  local copies, waits for them, and re-layouts  1.47 us (1%)
    pallas_call x1, Pallas kernels, per_device(): pl.pallas_call(kernel, out_shape=jax.ShapeDtypeStruct((32, 4, 128), f32),...  101 us

profile of v4, /device:TPU:1, one launch (start us, length us, event | category | flops | bytes accessed | tf_op | source)
XLA Modules:
  0.0 102.7 jit_solution(15546783356947326537)
XLA Ops:
  0.0 101.2 %doc_grads.1 = f32[32,4,128]{2,1,0:T(4,128)} custom-call(bf16[192,256]{1,0:T(8,128)(2,1)} %bitcast.11, bf16[192,256]{1,0:T(8,128)(2,1)} %bitcast.12, bf16[64,192]{1,0:T(8,128)(2,1)} %bitcast.14, bf16[64,501]{1,0:T(8,128)(2,1)} %bitcast.13, s32[2,128]{1,0:T(2,128)} %bitcast.15, s32[2,128]{1,0:T(2,128)} %bitcast.16, s32[2,128]{1,0:T(2,128)} %bitcast.17, ...), custom_call_target="tpu_custom_call" | custom-call | tf_op jit(solution)/shard_map/doc_grads/pallas_call | solution.py:579
  101.2 1.5 %copy.10 = f32[4,4096]{1,0:T(4,128)} copy(f32[4,4096]{1,0:T(4,128)} %bitcast.10) | data formatting | bytes 131072

commit v5 on v4

--- a/solution.py
+++ b/solution.py
@@ -19,11 +19,11 @@
 
 SCHEDULE = (
     ((1, 0, 0, 0), (
-        ("ZG", 1), ("CX",), ("ID",), ("ZG", 2), ("CZ", 0, 0, 1), ("CZ", 1, 0, 1), ("ZG", 3), ("CY", 2), ("CY", 1),
-        ("CY", 3), ("CZ", 0, 0, 2), ("CZ", 1, 0, 2), ("ZG", 4), ("SZ",), ("CZ", 1, 1, 1), ("S1", 0, 0), ("S1", 0, 1),
-        ("CZ", 0, 1, 1), ("S2", 1, 0, 0), ("S2", 1, 1, 0), ("S1", 1, 0), ("S1", 1, 1), ("P2",), ("LK", 0),
-        ("S2", 0, 0, 0), ("LK", 1), ("S2", 0, 1, 0), ("LK", 2), ("CZ", 1, 0, 3), ("CZ", 0, 0, 3), ("F1", 0, 0),
-        ("LK", 3), ("LS",), ("F1", 0, 1), ("CZ", 1, 2, 1), ("CZ", 0, 2, 1), ("F1", 1, 0), ("F1", 1, 1),
+        ("ZG", 1), ("CX",), ("ZG", 2), ("LK", 0), ("CZ", 0, 0, 1), ("CZ", 1, 0, 1), ("ZG", 3), ("LK", 1),
+        ("CY", 2), ("CY", 1), ("CY", 3), ("LK", 2), ("CZ", 0, 0, 2), ("CZ", 1, 0, 2), ("ZG", 4), ("SZ",), ("LK", 3),
+        ("LS",), ("CZ", 1, 1, 1), ("S1", 0, 0), ("S1", 0, 1), ("CZ", 0, 1, 1), ("S2", 1, 0, 0), ("S2", 1, 1, 0),
+        ("S1", 1, 0), ("S1", 1, 1), ("P2",), ("S2", 0, 0, 0), ("S2", 0, 1, 0), ("CZ", 1, 0, 3), ("CZ", 0, 0, 3),
+        ("F1", 0, 0), ("F1", 0, 1), ("CZ", 1, 2, 1), ("CZ", 0, 2, 1), ("F1", 1, 0), ("F1", 1, 1), ("EM",),
     )),
     ((2, 0, 0, 1), (
         ("F2", 1, 0, 0), ("F2", 1, 1, 0), ("CZ", 1, 1, 2), ("CZ", 0, 1, 2), ("CZ", 1, 0, 4), ("S2", 0, 0, 3),
@@ -87,11 +87,11 @@
 
 
 def kernel(
-    hid_ref, grad_ref, fp_ref, vp_ref, tgt_ref, ids_ref, docs_ref, emb_ref, out_ref,
-    hidv, rx, gath, hall_a, hall_bc, emb, pet, idb, part_a, part_bc, part_in_a, part_in_bc,
+    hid_in, grad_in, fp_in, vp_in, tgt_in, ids_in, docs_in, emb_ref, out_ref,
+    hid_ref, grad_ref, fp_ref, vp_ref, tgt_ref, ids_ref, docs_ref, hidv, rx, gath, hall_a, hall_bc, emb, pet, idb, part_a, part_bc, part_in_a, part_in_bc,
     look_a, look_bc, look_in_a, look_in_bc, look_q_a, look_q_bc, look_q_in_a, look_q_in_bc, look_z, look_z_in, found,
     far_in_a, far_in_bc, q1_a, q1_bc, q1_in_a, q1_in_bc, q2, q2_in, tok, emb_tok, feat, side, sd_in, sz, sz_in, turned,
-    sem_l, sem_c, sem_zg, sem_cx, sem_cz, sem_1, sem_2, sem_i, sem_s, sem_r, sem_f, sem_q, sem_t, sem_h,
+    sem_in, sem_l, sem_c, sem_zg, sem_cx, sem_cz, sem_1, sem_2, sem_i, sem_s, sem_r, sem_f, sem_q, sem_t, sem_h,
 ):
     g, v = lax.axis_index("dp"), lax.axis_index("vocab")
     x, y = lax.rem(g, 4), lax.div(g, 4)
@@ -136,14 +136,20 @@
     def outer(cls, k):
         return dev(dx=k) if cls == 1 else dev(dy=k)
 
+    sources = (hid_in, tgt_in, ids_in, vp_in, fp_in, grad_in, docs_in)
+    places = (hid_ref, tgt_ref, ids_ref, vp_ref, fp_ref, grad_ref, docs_ref)
+    loads = [pltpu.make_async_copy(src, dst, sem_in.at[n]) for n, (src, dst) in enumerate(zip(sources, places))]
+    for load in loads:
+        load.start()
     emb_local = pltpu.make_async_copy(emb_ref, emb.at[c], sem_l.at[0])
     emb_local.start()
     barrier = pltpu.get_barrier_semaphore()
     peers = [dev(dc=1)] + [dev(dz=k, dc=core) for k in range(1, 8) for core in (0, 1)]
-    peers += [dev(dx=k) for k in range(1, 4)] + [dev(dy=k) for k in range(1, 4)]
-    peers += [dev(dx=k, dy=2) for k in (1, 2, 3)] + [dev(dx=2, dy=k) for k in (1, 3)]
+    peers += [dev(dx=n % 4, dy=n // 4) for n in range(1, 16)]
     for peer in peers:
         pl.semaphore_signal(barrier, inc=1, device_id=peer, device_id_type=MESH)
+    for load in loads:
+        load.wait()
     first = c == 0
     hidv[...] = jnp.transpose(hid_ref[...].astype(jnp.float32)).astype(jnp.bfloat16)
     row_id = lax.broadcasted_iota(jnp.int32, (8, 128), 0)
@@ -178,11 +184,8 @@
     def emb_tok_swap():
         return remote(emb_tok.at[c], emb_tok.at[c], sem_c, (5,), dev(dc=1))
 
-    def ids_x(k):
-        return remote(idb.at[y, x], idb.at[y, x], sem_i, (0, k - 1), dev(dx=k))
-
-    def ids_y(k):
-        return remote(idb.at[y], idb.at[y], sem_i, (1, k - 1), dev(dy=k))
+    def ids_out(n):
+        return remote(idb.at[y, x], idb.at[y, x], sem_i, (n,), dev(dx=n % 4, dy=n // 4))
 
     def along_z(way, step):
         at = columns(z + 9 - step) if way == 0 else columns(z + step - 1)
@@ -281,9 +284,9 @@
         return remote(tok.at[c, z], tok.at[c, z], sem_h, (core, k), dev(dz=k, dc=core))
 
     go(hid_swap)
-    for k in (1, 2, 3):
-        go(ids_x, k)
     go(pet_swap)
+    for n in range(1, 16):
+        go(ids_out, n)
     hid_swap().wait_recv()
     own_half, got_half = hidv[pl.ds(mine, 128), :], rx[...]
     left = jnp.where(first, own_half, got_half)
@@ -391,11 +394,6 @@
                 held.setdefault(at[0], []).append(at)
         elif what == "F2":
             second_on(*at).wait_recv()
-        elif what == "ID":
-            for k in (1, 2, 3):
-                ids_x(k).wait_recv()
-            for k in (1, 2, 3):
-                go(ids_y, k)
         elif what == "SZ":
             side_swap().wait_recv()
             sz[...] = side[pl.ds(mine, 128), :] + sd_in[...]
@@ -415,8 +413,8 @@
         elif what == "LK":
             if at[0] == 0:
                 pet_swap().wait_recv()
-                for k in (1, 2, 3):
-                    ids_y(k).wait_recv()
+                for n in range(1, 16):
+                    ids_out(n).wait_recv()
 
             def one(gx, carry):
                 look_up(at[0], gx)
@@ -427,6 +425,7 @@
             for cls in (0, 1, 2):
                 for k in (1, 2, 3):
                     go(look_out, cls, k)
+        elif what == "EM":
             emb_local.wait()
             emb_swap().wait_recv()
             for copy in keep:
@@ -579,9 +578,16 @@
     out = pl.pallas_call(
         kernel,
         out_shape=jax.ShapeDtypeStruct((32, 4, 128), f32),
-        in_specs=[vmem] * 7 + [pl.BlockSpec(memory_space=pl.ANY)],
+        in_specs=[pl.BlockSpec(memory_space=pl.ANY)] * 8,
         out_specs=vmem,
         scratch_shapes=[
+            pltpu.VMEM((192, 256), bf16),
+            pltpu.VMEM((192, 256), bf16),
+            pltpu.VMEM((64, 192), bf16),
+            pltpu.VMEM((64, V_ROWS), bf16),
+            pltpu.VMEM((2, 128), i32),
+            pltpu.VMEM((2, 128), i32),
+            pltpu.VMEM((2, 128), i32),
             pltpu.VMEM((256, 192), bf16),
             pltpu.VMEM((128, 192), bf16),
             pltpu.VMEM((START[2], D), bf16),
@@ -621,6 +627,7 @@
             pltpu.VMEM((128, 128), f32),
             pltpu.VMEM((7, 16, 128), f32),
             pltpu.VMEM((2, 128, 128), f32),
+            dma((7,)),
             dma((3,)),
             dma((2, 6)),
             dma((2, 2, 4)),
@@ -628,7 +635,7 @@
             dma((2, 2, 4, 4)),
             dma((2, 2, 2, 2)),
             dma((2, 2, 2, 2, 4)),
-            dma((2, 2, 3)),
+            dma((2, 16)),
             dma((2, 3, 7)),
             dma((2, 2, 3, 3)),
             dma((2, 3, 4)),

time: 103 us -> 99.8 us (0.969)
  Pallas kernels: 101 us -> 98.2 us
    pallas_call x1, Pallas kernels: 101 us -> 98.2 us  [per_device(): pl.pallas_call(kernel, out_shape=jax.ShapeDtypeStruct((32, 4, 128), f32),...]
where the time goes in v5:
time: 99.8 us; the launch traced here: 99.6 us
  Pallas kernels  98.2 us (98%)
  local copies, waits for them, and re-layouts  1.47 us (1%)
    pallas_call x1, Pallas kernels, per_device(): pl.pallas_call(kernel, out_shape=jax.ShapeDtypeStruct((32, 4, 128), f32),...  98.2 us

profile of v5, /device:TPU:1, one launch (start us, length us, event | category | flops | bytes accessed | tf_op | source)
XLA Modules:
  0.0 99.6 jit_solution(10615960252722843305)
XLA Ops:
  0.0 98.2 %doc_grads.1 = f32[32,4,128]{2,1,0:T(4,128)} custom-call(bf16[192,256]{1,0:T(8,128)(2,1)} %bitcast.11, bf16[192,256]{1,0:T(8,128)(2,1)} %bitcast.12, bf16[64,192]{1,0:T(8,128)(2,1)} %bitcast.14, bf16[64,501]{1,0:T(8,128)(2,1)} %bitcast.13, s32[2,128]{1,0:T(2,128)} %bitcast.15, s32[2,128]{1,0:T(2,128)} %bitcast.16, s32[2,128]{1,0:T(2,128)} %bitcast.17, ...), custom_call_target="tpu_custom_call" | custom-call | tf_op jit(solution)/shard_map/doc_grads/pallas_call | solution.py:578
  98.2 1.5 %copy.10 = f32[4,4096]{1,0:T(4,128)} copy(f32[4,4096]{1,0:T(4,128)} %bitcast.10) | data formatting | bytes 131072

commit v6 on v5

--- a/solution.py
+++ b/solution.py
@@ -33,7 +33,7 @@
         ("CZ", 1, 2, 2), ("S2", 1, 0, 3), ("S2", 1, 1, 3), ("CZ", 0, 2, 2), ("S2", 0, 0, 1), ("S2", 0, 1, 1),
         ("CZ", 1, 1, 3), ("F2", 0, 0, 0), ("F2", 0, 1, 0), ("CZ", 0, 1, 3), ("CZ", 1, 3, 1), ("S2", 1, 0, 1),
         ("S2", 1, 1, 1), ("CZ", 0, 3, 1), ("S2", 0, 0, 2), ("S2", 0, 1, 2), ("CZ", 1, 2, 3), ("F2", 0, 0, 3),
-        ("F2", 0, 1, 3), ("CZ", 0, 2, 3), ("CZ", 1, 1, 4), ("CZ", 0, 1, 4), ("F2", 0, 0, 1),
+        ("F2", 0, 1, 3), ("CZ", 0, 2, 3), ("CZ", 1, 1, 4), ("CZ", 0, 1, 4), ("F2", 0, 0, 1), ("L1",),
     )),
     ((1, 1, 1, 1), (
         ("F2", 0, 1, 1), ("S2", 1, 0, 2), ("S2", 1, 1, 2), ("CZ", 1, 3, 2), ("F2", 0, 0, 2), ("F2", 0, 1, 2),
@@ -43,13 +43,13 @@
         ("CZ", 1, 2, 4), ("F2", 1, 0, 3), ("F2", 1, 1, 3), ("CZ", 0, 2, 4), ("FE",),
     )),
     ((2, 3, 3, 1), (
-        ("F2", 1, 0, 1), ("F2", 1, 1, 1), ("CZ", 1, 3, 3), ("CZ", 0, 3, 3), ("L1",),
+        ("F2", 1, 0, 1), ("F2", 1, 1, 1), ("CZ", 1, 3, 3), ("CZ", 0, 3, 3), ("L2",),
     )),
     ((1, 2, 2, 0), (
         ("F2", 1, 0, 2), ("F2", 1, 1, 2),
     )),
     ((2, 2, 2, 1), (
-        ("CZ", 1, 3, 4), ("CZ", 0, 3, 4), ("L2",), ("FW",), ("FIN", 1),
+        ("CZ", 1, 3, 4), ("CZ", 0, 3, 4), ("FW",), ("L3",), ("FIN", 1),
     )),
 )
 

time: 99.8 us -> 99.8 us (level)
  no operation moved by 1% of the time
where the time goes in v6:
time: 99.8 us; the launch traced here: 99.7 us
  Pallas kernels  98.2 us (98%)
  local copies, waits for them, and re-layouts  1.47 us (1%)
    pallas_call x1, Pallas kernels, per_device(): pl.pallas_call(kernel, out_shape=jax.ShapeDtypeStruct((32, 4, 128), f32),...  98.2 us

profile of v6, /device:TPU:1, one launch (start us, length us, event | category | flops | bytes accessed | tf_op | source)
XLA Modules:
  0.0 99.7 jit_solution(725038301748490183)
XLA Ops:
  0.0 98.2 %doc_grads.1 = f32[32,4,128]{2,1,0:T(4,128)} custom-call(bf16[192,256]{1,0:T(8,128)(2,1)} %bitcast.11, bf16[192,256]{1,0:T(8,128)(2,1)} %bitcast.12, bf16[64,192]{1,0:T(8,128)(2,1)} %bitcast.14, bf16[64,501]{1,0:T(8,128)(2,1)} %bitcast.13, s32[2,128]{1,0:T(2,128)} %bitcast.15, s32[2,128]{1,0:T(2,128)} %bitcast.16, s32[2,128]{1,0:T(2,128)} %bitcast.17, ...), custom_call_target="tpu_custom_call" | custom-call | tf_op jit(solution)/shard_map/doc_grads/pallas_call | solution.py:578
  98.2 1.5 %copy.10 = f32[4,4096]{1,0:T(4,128)} copy(f32[4,4096]{1,0:T(4,128)} %bitcast.10) | data formatting | bytes 131072
